TPU v7x, 128 devices: a whole 4x4x4 slice. The times are simulated.
128 devices in a mesh: row: 8 (over y, core), col: 16 (over z, x).
Axes of the slice: x: 4, y: 4, z: 4, core: 2. Of those that a mesh axis runs over, the one named last changes fastest.
Arguments:
- a_blocks: bfloat16 [8, 512, 64, 1728], P('row', 'col'), may hold values from -0.75 to 0.75
- a_cols: int32 [8, 512, 27], P('row', 'col'), may hold values from 0 to 47
- p_blocks: bfloat16 [8, 64, 32768], P('row', None, 'col'), may hold values from -2.09375 to 2.09375
- contrib_peer: int32 [8, 13824], P('row', 'col'), may hold values from 0 to 15
- contrib_slot: int32 [8, 13824], P('row', 'col'), may hold values from 0 to 53
- outbound_term_lists: int32 [8, 256, 13], P('row', 'col'), may hold values from 0 to 863, as said below
- send_count: int32 [8, 256], P('row', 'col'), may hold values from 0 to 13, as said below
- keep: int32 [8], replicated, may hold values from 0 to 1, as said below
Outputs:
- coarse: float32 [8, 64, 55296], P('row', None, 'col')
Inputs may be any that keep to these rules, and one draw needn't show every extreme that they name: keep[r] + keep[r2] = 1 for rows r and r2 half the row axis apart. `send_count`: a device's count for its own column is 0; in each row of devices one column gets exactly 13 terms from every other device of that row. `outbound_term_lists`: entries 0 to send_count[p] - 1 of list p of a device name, each once, exactly its terms e with contrib_peer[e] = p; later entries are arbitrary; every term whose contrib_peer differs from the device's column is listed.
All inputs are finite; a program needn't handle non-finite values.
Results may differ from a plain program's by a relative error of at most 0.0041.
Values may be sent and summed in bfloat16 or wider, within the bound.
A program may use at most 192 MiB of HBM per device.

v0:
```python
import jax
import jax.numpy as jnp
from jax import lax
from jax.sharding import PartitionSpec as P

H = 8
CS = 54


def from_partner(value, axis, apart):
    mask = 2**apart
    pairs = [(source, source ^ mask) for source in range(lax.axis_size(axis))]
    return lax.ppermute(value, axis, pairs)


def extended(cells, sides, width):
    for axis, dim in sides:
        count = lax.axis_size(axis)
        ends = count - 1
        head = lax.slice_in_dim(cells, 0, width, axis=dim)
        tail = lax.slice_in_dim(cells, cells.shape[dim] - width, cells.shape[dim], axis=dim)
        cells = jnp.concatenate(
            [
                lax.ppermute(tail, axis, [(i, (i + 1) % count) for i in range(ends)]),
                cells,
                lax.ppermute(head, axis, [((i + 1) % count, i) for i in range(ends)]),
            ],
            axis=dim,
        )
    return cells


def block_terms(operator_row_blocks, block_cols, prolong_rows, rim_table):
    fine_rows = operator_row_blocks.shape[0]
    block_width = prolong_rows.shape[0]
    depth = block_cols.shape[1]
    table_blocks = (
        rim_table.reshape(block_width, -1, block_width)
        .transpose(1, 0, 2)
        .reshape(-1, block_width * block_width)
    )
    table_count = table_blocks.shape[0]
    selector = (
        block_cols.reshape(-1)[:, None] == jnp.arange(table_count, dtype=jnp.int32)[None, :]
    ).astype(jnp.bfloat16)
    picked = jnp.dot(selector, table_blocks, preferred_element_type=jnp.float32).astype(
        jnp.bfloat16
    )
    picked = picked.reshape(fine_rows, depth, block_width, block_width)
    a_split = operator_row_blocks.reshape(fine_rows, block_width, depth, block_width)
    product = jnp.einsum(
        "iakb,ikbc->ikac", a_split, picked, preferred_element_type=jnp.float32
    ).astype(jnp.bfloat16)
    prolong_own = prolong_rows.reshape(block_width, fine_rows, block_width)
    galerkin = jnp.einsum(
        "bia,ikbc->ikac", prolong_own, product, preferred_element_type=jnp.float32
    )
    return galerkin.astype(jnp.bfloat16).reshape(fine_rows * depth, block_width * block_width)


def slot_sum(values, slot_ids, count_slots):
    onehot = (jnp.arange(count_slots, dtype=jnp.int32)[:, None] == slot_ids[None, :]).astype(
        jnp.bfloat16
    )
    return jnp.dot(onehot, values, preferred_element_type=jnp.float32)


def listed(listed_items, row_term_count):
    return jnp.arange(listed_items.shape[-1], dtype=jnp.int32)[None, :] < row_term_count[:, None]


def on_device(
    a_blocks, a_cols, p_blocks, contrib_peer, contrib_slot, outbound_term_lists, send_count, keep
):
    block_width = p_blocks.shape[1]
    columns = lax.axis_size("col")
    partner_bit = lax.axis_size("row").bit_length() - 2
    retained_device = keep[lax.axis_index("row")] == 1
    own_col = lax.axis_index("col")
    item_total = a_cols.shape[1] * a_cols.shape[2]
    partner = from_partner(
        (a_blocks, a_cols, p_blocks, contrib_peer, contrib_slot, outbound_term_lists, send_count),
        "row",
        partner_bit,
    )
    merged_prolong = jnp.concatenate([p_blocks, partner[2]], axis=0)
    rim_table = extended(merged_prolong, (("col", 2),), H * block_width)
    galerkin = jnp.concatenate(
        [
            block_terms(a_blocks[0], a_cols[0], p_blocks[0], rim_table[0]),
            block_terms(partner[0][0], partner[1][0], partner[2][0], rim_table[1]),
        ],
        axis=0,
    )
    slot_ids = jnp.concatenate([contrib_slot[0], partner[4][0]])
    owner_cols = jnp.concatenate([contrib_peer[0], partner[3][0]])
    listed_items = jnp.concatenate([outbound_term_lists[0], partner[5][0] + item_total], axis=1)
    active_term_mask = jnp.concatenate(
        [listed(outbound_term_lists[0], send_count[0]), listed(partner[5][0], partner[6][0])],
        axis=1,
    )
    active_term_mask = jnp.logical_and(active_term_mask, retained_device)
    local_partial_sum = slot_sum(galerkin, jnp.where(owner_cols == own_col, slot_ids, CS), CS)
    flat_items = listed_items.reshape(-1)
    flat_live = active_term_mask.reshape(-1)
    term_range = jnp.arange(galerkin.shape[0], dtype=jnp.int32)
    chooser = jnp.logical_and(
        flat_items[:, None] == term_range[None, :], flat_live[:, None]
    ).astype(jnp.bfloat16)
    outgoing = jnp.dot(chooser, galerkin, preferred_element_type=jnp.float32).astype(jnp.bfloat16)
    outgoing = outgoing.reshape(columns, -1, block_width * block_width)
    out_slots = jnp.where(flat_live, slot_ids[flat_items], CS).reshape(columns, -1)
    arrived, arrived_slots = (
        lax.all_to_all(outgoing, "col", split_axis=0, concat_axis=0, tiled=True),
        lax.all_to_all(out_slots, "col", split_axis=0, concat_axis=0, tiled=True),
    )
    received_partial_sum = slot_sum(
        arrived.reshape(-1, block_width * block_width), arrived_slots.reshape(-1), CS
    )
    coarse = jnp.where(retained_device, local_partial_sum + received_partial_sum, jnp.float32(0.0))
    coarse = coarse.reshape(CS, block_width, block_width).transpose(1, 0, 2)
    return coarse.reshape(1, block_width, CS * block_width)


def solution(mesh):
    placed = (
        P("row", "col", None, None),
        P("row", "col", None),
        P("row", None, "col"),
        P("row", "col"),
        P("row", "col"),
        P("row", "col", None),
        P("row", "col"),
        P(),
    )
    return jax.shard_map(
        on_device, mesh=mesh, in_specs=placed, out_specs=P("row", None, "col"), check_vma=False
    )
```

profile of v0, /device:TPU:0, one launch (start us, length us, event | category | flops | bytes accessed | tf_op | source)
XLA Modules:
  0.0 484.7 jit_solution(2314023922194543310)
XLA Ops:
  0.0 3.4 collective-permute-start.6
  3.4 0.2 collective-permute-start.2
  3.6 3.3 collective-permute-start.5
  6.9 0.2 collective-permute-start.7
  7.2 3.3 collective-permute-start.8
  10.5 0.8 copy.38
  11.2 22.7 %reshape_squeeze.19 = bf16[32,64,27,64]{3,2,1,0:T(8,128)(2,1)} reshape(bf16[1,32,64,1728]{3,2,1,0:T(8,128)(2,1)} %param.8) | data formatting | bytes 14155776 | tf_op jit(solution)/shard_map/reshape;squeeze | solution.py:50
  34.0 0.5 reshape_squeeze.20
  34.5 0.1 eq.96
  34.7 0.6 dynamic_slice.3
  35.3 0.1 fusion.40
  36.0 131.6 %collective-permute-done.7 = s32[1,16]{1,0:T(1,128)S(1)} collective-permute-done((s32[1,16]{1,0:T(1,128)}, s32[1,16]{1,0:T(1,128)S(1)}, u32[]{:S(2)}, u32[]{:S(2)}) %collective-permute-start.7) | collective-permute-done | bytes 96 | tf_op jit(solution)/shard_map/ppermute | solution.py:13
  167.6 3.2 collective-permute-start
  170.9 0.1 fusion.41
  171.0 0.1 add_and_fusion.1
  171.0 0.1 and.40
  171.2 0.4 collective-permute-start.1
  171.6 0.1 copy.50
  171.6 0.1 reshape.190
  171.8 0.1 eq.108
  171.8 0.1 copy.44
  171.9 0.1 eq.100
  172.0 0.7 collective-permute-done
  172.8 3.6 collective-permute-done.1
  176.4 0.1 pad_add_fusion.1
  176.4 2.8 gather_fusion
  179.3 0.1 gather.6
  179.4 3.4 collective-permute-start.3
  182.8 1.3 collective-permute-start.4
  184.1 0.7 fusion.39
  184.8 9.0 %all-to-all-start = ((s32[16,1,26]{2,1,0:T(1,128)}), s32[16,1,26]{2,1,0:T(1,128)S(1)}, u32[]{:S(2)}, u32[]{:S(2)}) async-start(s32[16,1,26]{2,1,0:T(1,128)} %bitcast.14), calls=%async_computation | async-start | bytes 16384 | tf_op jit(solution)/shard_map/all_to_all | solution.py:115
  193.9 0.5 reshape_squeeze.23
  194.5 0.5 reshape_squeeze.21
  195.0 0.2 copy.90
  195.2 0.6 reshape.187
  195.9 5.0 %convolution_convert_fusion = bf16[864,4096]{1,0:T(8,128)(2,1)} fusion(bf16[48,4096]{1,0:T(8,128)(2,1)S(1)} %reshape.187, s32[864]{0:T(1024)S(1)} %eq.100), kind=kOutput, calls=%fused_computation.13 | convolution fusion | flops 343319040 | bytes 7474560 | tf_op jit(solution)/shard_map/dot_general | solution.py:46
  200.9 20.0 %reshape.188 = bf16[32,27,64,64]{3,2,1,0:T(8,128)(2,1)} reshape(bf16[864,4096]{1,0:T(8,128)(2,1)} %convolution_convert_fusion) | data formatting | bytes 14155776 | tf_op jit(solution)/shard_map/reshape | solution.py:49
  220.9 0.5 reshape_squeeze.18
  221.4 0.2 copy.91
  221.6 0.6 reshape.184
  222.2 4.9 %convolution_convert_fusion.1 = bf16[864,4096]{1,0:T(8,128)(2,1)} fusion(bf16[48,4096]{1,0:T(8,128)(2,1)S(1)} %reshape.184, s32[864]{0:T(1024)S(1)} %eq.96), kind=kOutput, calls=%fused_computation.14 | convolution fusion | flops 343319040 | bytes 7474560 | tf_op jit(solution)/shard_map/dot_general | solution.py:46
  227.2 19.9 %reshape.185 = bf16[32,27,64,64]{3,2,1,0:T(8,128)(2,1)} reshape(bf16[864,4096]{1,0:T(8,128)(2,1)} %convolution_convert_fusion.1) | data formatting | bytes 14155776 | tf_op jit(solution)/shard_map/reshape | solution.py:49
  247.1 20.0 %convert_bitcast_fusion.1 = bf16[32,27,64,64]{2,3,1,0:T(8,128)(2,1)} fusion(bf16[32,27,64,64]{3,2,1,0:T(8,128)(2,1)} %reshape.185, bf16[32,64,27,64]{3,2,1,0:T(8,128)(2,1)} %reshape_squeeze.19, bf16[64,32,64,1]{2,1,0,3:T(8,128)(2,1)S(1)} %bitcast.58), kind=kOutput, calls=%fused_computation.11 | convolution fusion | flops 913047552 | bytes 21495808 | tf_op jit(solution)/shard_map/bia,ikbc->ikac/dot_general | solution.py:55
  267.1 18.8 %copy.43 = bf16[32,27,64,64]{3,2,1,0:T(8,128)(2,1)} copy(bf16[32,27,64,64]{2,3,1,0:T(8,128)(2,1)} %convert_bitcast_fusion.1) | data formatting | bytes 14155776 | tf_op jit(solution)/shard_map/convert_element_type | solution.py:58
  285.9 19.0 %reshape.186 = bf16[864,4096]{1,0:T(8,128)(2,1)} reshape(bf16[32,27,64,64]{3,2,1,0:T(8,128)(2,1)} %copy.43) | data formatting | bytes 14155776 | tf_op jit(solution)/shard_map/reshape | solution.py:58
  304.9 6.9 %constant_dynamic-update-slice_fusion.3 = bf16[1728,4096]{1,0:T(8,128)(2,1)} fusion(bf16[864,4096]{1,0:T(8,128)(2,1)} %reshape.186), kind=kLoop, calls=%fused_computation.44 | loop fusion | bytes 14155776
  311.8 22.7 %reshape_squeeze.22 = bf16[32,64,27,64]{3,2,1,0:T(8,128)(2,1)} reshape(bf16[1,32,64,1728]{3,2,1,0:T(8,128)(2,1)} %collective-permute-done.6) | data formatting | bytes 14155776 | tf_op jit(solution)/shard_map/reshape;squeeze | solution.py:50
  334.5 20.0 %convert_bitcast_fusion = bf16[32,27,64,64]{2,3,1,0:T(8,128)(2,1)} fusion(bf16[32,27,64,64]{3,2,1,0:T(8,128)(2,1)} %reshape.188, bf16[32,64,27,64]{3,2,1,0:T(8,128)(2,1)} %reshape_squeeze.22, bf16[64,32,64,1]{2,1,0,3:T(8,128)(2,1)S(1)} %bitcast.59), kind=kOutput, calls=%fused_computation.9 | convolution fusion | flops 913047552 | bytes 21495808 | tf_op jit(solution)/shard_map/bia,ikbc->ikac/dot_general | solution.py:55
  354.6 18.8 %copy.49 = bf16[32,27,64,64]{3,2,1,0:T(8,128)(2,1)} copy(bf16[32,27,64,64]{2,3,1,0:T(8,128)(2,1)} %convert_bitcast_fusion) | data formatting | bytes 14155776 | tf_op jit(solution)/shard_map/convert_element_type | solution.py:58
  373.3 19.0 %reshape.189 = bf16[864,4096]{1,0:T(8,128)(2,1)} reshape(bf16[32,27,64,64]{3,2,1,0:T(8,128)(2,1)} %copy.49) | data formatting | bytes 14155776 | tf_op jit(solution)/shard_map/reshape | solution.py:58
  392.3 6.8 %constant_dynamic-update-slice_fusion.2 = bf16[1728,4096]{1,0:T(8,128)(2,1)} fusion(bf16[1728,4096]{1,0:T(8,128)(2,1)} %constant_dynamic-update-slice_fusion.3, bf16[864,4096]{1,0:T(8,128)(2,1)} %reshape.189), kind=kLoop, calls=%fused_computation.43 | loop fusion | bytes 14155776 | tf_op jit(solution)/shard_map/concatenate | solution.py:88
  399.1 9.6 %convolution_convert_fusion.2 = bf16[416,4096]{1,0:T(8,128)(2,1)S(1)} fusion(bf16[1728,4096]{1,0:T(8,128)(2,1)} %constant_dynamic-update-slice_fusion.2, s32[416]{0:T(512)S(1)} %eq.108, pred[416]{0:T(512)(128)(4,1)S(1)} %and.40), kind=kOutput, calls=%fused_computation.15 | convolution fusion | flops 5891944448 | bytes 17565728 | tf_op jit(solution)/shard_map/dot_general | solution.py:110
  408.7 2.9 reshape.191
  411.5 7.3 %all-to-all-start.1 = ((bf16[16,26,4096]{2,1,0:T(8,128)(2,1)}), bf16[16,26,4096]{2,1,0:T(8,128)(2,1)}, u32[]{:S(2)}, u32[]{:S(2)}) async-start(bf16[16,26,4096]{2,1,0:T(8,128)(2,1)} %reshape.191), calls=%async_computation.1 | async-start | bytes 8388608 | tf_op jit(solution)/shard_map/all_to_all | solution.py:114
  418.8 0.5 broadcast.70
  419.3 0.7 reduce.7
  420.0 0.1 eq.105
  420.1 8.6 %fusion.33 = f32[54,4096]{1,0:T(8,128)} fusion(bf16[1728,4096]{1,0:T(8,128)(2,1)} %constant_dynamic-update-slice_fusion.2, s32[1728]{0:T(1024)S(1)} %get-tuple-element.10), kind=kOutput, calls=%fused_computation.31 | convolution fusion | flops 764505216 | bytes 15047424 | tf_op jit(solution)/shard_map/dot_general | solution.py:65
  428.7 42.8 %all-to-all-done.1 = bf16[16,26,4096]{2,1,0:T(8,128)(2,1)} async-done(((bf16[16,26,4096]{2,1,0:T(8,128)(2,1)}), bf16[16,26,4096]{2,1,0:T(8,128)(2,1)}, u32[]{:S(2)}, u32[]{:S(2)}) %all-to-all-start.1) | async-done | bytes 3407904 | tf_op jit(solution)/shard_map/all_to_all | solution.py:114
  471.6 3.4 reshape.192
  474.9 2.9 fusion.26
  477.8 3.0 reshape.193
  480.8 2.5 copy.89
  483.3 1.3 reshape.194
  (34 shorter events, 0.3 us)
Async XLA Ops:
  0.0 34.0 %copy-start = (bf16[1,64,2048]{2,1,0:T(8,128)(2,1)S(1)}, bf16[1,64,2048]{2,1,0:T(8,128)(2,1)}, u32[]{:S(2)}) copy-start(bf16[1,64,2048]{2,1,0:T(8,128)(2,1)} %param.10) | copy-start | bytes 786436
  0.0 35.3 %copy-start.4 = (s32[1,16]{1,0:T(1,128)S(1)}, s32[1,16]{1,0:T(1,128)}, u32[]{:S(2)}) copy-start(s32[1,16]{1,0:T(1,128)} %param.14) | copy-start | bytes 196
  0.0 34.5 %copy-start.1 = (s32[1,16,13]{1,0,2:T(1,128)S(1)}, s32[1,16,13]{1,0,2:T(1,128)}, u32[]{:S(2)}) copy-start(s32[1,16,13]{1,0,2:T(1,128)} %param.13) | copy-start | bytes 2500
  0.0 34.6 %copy-start.2 = (s32[1,864]{1,0:T(1,128)S(1)}, s32[1,864]{1,0:T(1,128)}, u32[]{:S(2)}) copy-start(s32[1,864]{1,0:T(1,128)} %param.11) | copy-start | bytes 10372
  0.0 34.7 %copy-start.3 = (s32[1,864]{1,0:T(1,128)S(1)}, s32[1,864]{1,0:T(1,128)}, u32[]{:S(2)}) copy-start(s32[1,864]{1,0:T(1,128)} %param.12) | copy-start | bytes 10372
  0.0 34.7 %copy-start.5 = (s32[8]{0:T(128)S(1)}, s32[8]{0:T(128)}, u32[]{:S(2)}) copy-start(s32[8]{0:T(128)} %param.15) | copy-start | bytes 100
  0.0 311.8 %collective-permute-start.6 = (bf16[1,32,64,1728]{3,2,1,0:T(8,128)(2,1)}, bf16[1,32,64,1728]{3,2,1,0:T(8,128)(2,1)}, u32[]{:S(2)}, u32[]{:S(2)}) collective-permute-start(bf16[1,32,64,1728]{3,2,1,0:T(8,128)(2,1)} %param.8), channel_id=1, source_target_pairs={{0,64},{16,80},{32,96},{48,112},{64,0},{80,16},{96,32},{112,48},{1... | collective-permute-start | bytes 21233672 | tf_op jit(solution)/shard_map/ppermute | solution.py:13
  3.4 176.0 %collective-permute-start.2 = (bf16[1,64,2048]{2,1,0:T(8,128)(2,1)}, bf16[1,64,2048]{2,1,0:T(8,128)(2,1)S(1)}, u32[]{:S(2)}, u32[]{:S(2)}) collective-permute-start(bf16[1,64,2048]{2,1,0:T(8,128)(2,1)} %param.10), channel_id=1, source_target_pairs={{0,64},{16,80},{32,96},{48,112},{64,0},{80,16},{96,32},{112,48},{1... | collective-permute-start | bytes 786440 | tf_op jit(solution)/shard_map/ppermute | solution.py:13
  3.6 168.2 %collective-permute-start.5 = (s32[1,32,27]{1,0,2:T(1,128)}, s32[1,32,27]{1,0,2:T(1,128)S(1)}, u32[]{:S(2)}, u32[]{:S(2)}) collective-permute-start(s32[1,32,27]{1,0,2:T(1,128)} %param.9), channel_id=1, source_target_pairs={{0,64},{16,80},{32,96},{48,112},{64,0},{80,16},{96,32},{112,48},{1... | collective-permute-start | bytes 10376 | tf_op jit(solution)/shard_map/ppermute | solution.py:13
  6.9 160.7 %collective-permute-start.7 = (s32[1,16]{1,0:T(1,128)}, s32[1,16]{1,0:T(1,128)S(1)}, u32[]{:S(2)}, u32[]{:S(2)}) collective-permute-start(s32[1,16]{1,0:T(1,128)} %param.14), channel_id=1, source_target_pairs={{0,64},{16,80},{32,96},{48,112},{64,0},{80,16},{96,32},{112,48},{1... | collective-permute-start | bytes 200 | tf_op jit(solution)/shard_map/ppermute | solution.py:13
  7.2 164.0 %collective-permute-start.8 = (s32[1,16,13]{1,0,2:T(1,128)}, s32[1,16,13]{1,0,2:T(1,128)S(1)}, u32[]{:S(2)}, u32[]{:S(2)}) collective-permute-start(s32[1,16,13]{1,0,2:T(1,128)} %param.13), channel_id=1, source_target_pairs={{0,64},{16,80},{32,96},{48,112},{64,0},{80,16},{96,32},{112,48},{1... | collective-permute-start | bytes 2504 | tf_op jit(solution)/shard_map/ppermute | solution.py:13
  167.6 5.1 %collective-permute-start = (s32[1,864]{1,0:T(1,128)S(1)}, s32[1,864]{1,0:T(1,128)S(1)}, u32[]{:S(2)}, u32[]{:S(2)}) collective-permute-start(s32[1,864]{1,0:T(1,128)S(1)} %copy-done.2), channel_id=1, source_target_pairs={{0,64},{16,80},{32,96},{48,112},{64,0},{80,16},{96,32},{112,48},{1... | collective-permute-start | bytes 10376 | tf_op jit(solution)/shard_map/ppermute | solution.py:13
  171.2 5.2 %collective-permute-start.1 = (s32[1,864]{1,0:T(1,128)S(1)}, s32[1,864]{1,0:T(1,128)S(1)}, u32[]{:S(2)}, u32[]{:S(2)}) collective-permute-start(s32[1,864]{1,0:T(1,128)S(1)} %copy-done.3), channel_id=1, source_target_pairs={{0,64},{16,80},{32,96},{48,112},{64,0},{80,16},{96,32},{112,48},{1... | collective-permute-start | bytes 10376 | tf_op jit(solution)/shard_map/ppermute | solution.py:13
  179.4 15.0 %collective-permute-start.3 = (bf16[2,64,512]{2,1,0:T(8,128)(2,1)S(1)}, bf16[2,64,512]{2,1,0:T(8,128)(2,1)S(1)}, u32[]{:S(2)}, u32[]{:S(2)}) collective-permute-start(bf16[2,64,512]{2,1,0:T(8,128)(2,1)S(1)} %get-tuple-element.7), channel_id=1, source_target_pairs={{0,1},{1,2},{2,3},{3,4},{4,5},{5,6},{6,7},{7,8},{8,9},{9,10},{10,1... | collective-permute-start | bytes 393224 | tf_op jit(solution)/shard_map/ppermute | solution.py:24
  182.8 11.6 %collective-permute-start.4 = (bf16[2,64,512]{2,1,0:T(8,128)(2,1)S(1)}, bf16[2,64,512]{2,1,0:T(8,128)(2,1)S(1)}, u32[]{:S(2)}, u32[]{:S(2)}) collective-permute-start(bf16[2,64,512]{2,1,0:T(8,128)(2,1)S(1)} %get-tuple-element.8), channel_id=1, source_target_pairs={{1,0},{2,1},{3,2},{4,3},{5,4},{6,5},{7,6},{8,7},{9,8},{10,9},{11,1... | collective-permute-start | bytes 393224 | tf_op jit(solution)/shard_map/ppermute | solution.py:26
  184.8 226.7 %all-to-all-start = ((s32[16,1,26]{2,1,0:T(1,128)}), s32[16,1,26]{2,1,0:T(1,128)S(1)}, u32[]{:S(2)}, u32[]{:S(2)}) async-start(s32[16,1,26]{2,1,0:T(1,128)} %bitcast.14), calls=%async_computation | async-start | bytes 16384 | tf_op jit(solution)/shard_map/all_to_all | solution.py:115
  411.5 60.0 %all-to-all-start.1 = ((bf16[16,26,4096]{2,1,0:T(8,128)(2,1)}), bf16[16,26,4096]{2,1,0:T(8,128)(2,1)}, u32[]{:S(2)}, u32[]{:S(2)}) async-start(bf16[16,26,4096]{2,1,0:T(8,128)(2,1)} %reshape.191), calls=%async_computation.1 | async-start | bytes 8388608 | tf_op jit(solution)/shard_map/all_to_all | solution.py:114
where the time goes:
time: 489 us; the launch traced here: 485 us
  local copies, waits for them, and re-layouts  197 us (40%)
  waiting for transfers between devices  179 us (37%)
  matrix products  71.1 us (15%)
  starting transfers between devices  35.1 us (7%)
    ppermute x7, waiting for transfers between devices, from_partner(): return lax.ppermute(value, axis, pairs)  136 us
    another operation x2, local copies, waits for them, and re-layouts, block_terms(): operator_row_blocks.reshape(fine_rows, block_width, depth, block_width)  45.5 us
    all_to_all x1, waiting for transfers between devices, on_device(): lax.all_to_all(outgoing, 'col', split_axis=0, concat_axis=0, tiled=True)  42.8 us
    dot_general x2, matrix products, block_terms(): jnp.einsum('bia,ikbc->ikac', prolong_own, product, preferred_element_type...  40 us
    reshape x2, local copies, waits for them, and re-layouts, block_terms(): picked = picked.reshape(fine_rows, depth, block_width, block_width)  39.9 us
    reshape x2, local copies, waits for them, and re-layouts, block_terms(): galerkin.astype(jnp.bfloat16)  38 us
    convert_element_type x2, local copies, waits for them, and re-layouts, block_terms(): galerkin.astype(jnp.bfloat16)  37.6 us
    ppermute x7, starting transfers between devices, from_partner(): return lax.ppermute(value, axis, pairs)  14 us
  transfers between devices with their start and end apart: 11, of which 4 were waited for; matrix products, arithmetic and copies ran while one was open for 53% of the time, Pallas kernels for 0%

commit v1 on v0

v1 whole, which is shorter than its diff:
```python
import functools

import jax
import jax.numpy as jnp
from jax import lax
from jax.experimental import pallas as pl
from jax.experimental.pallas import tpu as pltpu
from jax.sharding import PartitionSpec as P

B = 64
KA = 27
FB = 32
H = 8
CAP = 13
CS = 54
N_COL = 16
KP = 14
GROUP = 4

F32 = jnp.float32
BF16 = jnp.bfloat16
VM = pltpu.VMEM
SM = pltpu.SMEM


def left_half(shape):
    return lax.broadcasted_iota(jnp.int32, shape, len(shape) - 1) < B


def q_kernel(p_ref, a_ref, q_ref):
    for ii in range(GROUP):
        p = p_ref[:, ii * B : (ii + 1) * B]
        q = lax.dot_general(p, a_ref[ii], (((0,), (0,)), ((), ())), preferred_element_type=F32)
        q_ref[ii, :, : KA * B] = q.astype(BF16)
        q_ref[ii, :, KA * B :] = jnp.zeros((B, B), BF16)


def fill_table(table_ref, pieces):
    at = 0
    for ref, tiles in pieces:
        for m in range(tiles):
            tile = ref[:, m * 2 * B : (m + 1) * 2 * B].astype(F32)
            turned = pltpu.roll(tile, B, 1)
            low = left_half(tile.shape)
            table_ref[at] = jnp.where(low, tile, turned).astype(BF16)
            table_ref[at + 1] = jnp.where(low, turned, tile).astype(BF16)
            at += 2


def packed(pair):
    return jnp.where(left_half((B // 2, 2 * B)), pair[: B // 2], pair[B // 2 :])


def listed_kernel(items, counts, slots, cols, q_ref, p_ref, left_ref, right_ref, out_ref, table_ref, slot_ref):
    fill_table(table_ref, ((left_ref, H // 2), (p_ref, FB // 2), (right_ref, H // 2)))
    zero = jnp.zeros((B, 2 * B), BF16)

    @pl.loop(0, N_COL)
    def _(p):
        for j in range(CAP):
            e = items[p, j]
            live = j < counts[p]
            i = e // KA
            k = e - i * KA
            kp = k // 2
            odd = (k - 2 * kp) == 1
            tile = q_ref[i, :, pl.ds(pl.multiple_of(kp * 2 * B, 2 * B), 2 * B)]
            t = table_ref[cols[i, k]]
            rhs = jnp.concatenate([jnp.where(odd, zero, t), jnp.where(odd, t, zero)], axis=0)
            g = jnp.dot(tile, rhs, preferred_element_type=F32)
            out_ref[p, j] = packed(g).astype(BF16)
            slot_ref[p, j] = jnp.where(live, slots[i, k], CS)


def local_kernel(slots, cols, q_ref, table_ref, even_ref, odd_ref):
    even_ref[...] = jnp.zeros_like(even_ref)
    odd_ref[...] = jnp.zeros_like(odd_ref)
    zero = jnp.zeros((B, 2 * B), BF16)

    @pl.loop(0, FB)
    def _(i):
        for kp in range(KP):
            tile = q_ref[i, :, kp * 2 * B : (kp + 1) * 2 * B]
            k0 = 2 * kp
            k1 = 2 * kp + 1
            t0 = table_ref[cols[i, k0]]
            if k1 < KA:
                t1 = table_ref[cols[i, k1]]
                rhs = jnp.concatenate(
                    [jnp.concatenate([t0, zero], axis=1), jnp.concatenate([zero, t1], axis=1)], axis=0
                )
            else:
                rhs = jnp.concatenate([t0, zero], axis=0)
            g = jnp.dot(tile, rhs, preferred_element_type=F32)
            even_ref[slots[i, k0]] += packed(g[:, : 2 * B])
            if k1 < KA:
                odd_ref[slots[i, k1]] += packed(g[:, 2 * B :])


def merge_kernel(slots, even_ref, odd_ref, arrived_ref, acc_ref, sent_ref, work):
    work[...] = even_ref[...]

    @pl.loop(0, N_COL)
    def _(p):
        for j in range(CAP):
            work[slots[p, j]] += arrived_ref[p, j].astype(F32)

    @pl.loop(0, CS)
    def _(s):
        total = work[s] + odd_ref[s]
        acc_ref[s] = total
        sent_ref[s] = total.astype(BF16)


def final_kernel(keep, acc_ref, partner_ref, out_ref):
    weight = keep[0].astype(F32)
    low = left_half((B // 2, 2 * B))
    for m in range(CS // 2):
        a = (acc_ref[2 * m] + partner_ref[2 * m].astype(F32)) * weight
        b = (acc_ref[2 * m + 1] + partner_ref[2 * m + 1].astype(F32)) * weight
        lanes = slice(m * 2 * B, (m + 1) * 2 * B)
        out_ref[0, : B // 2, lanes] = jnp.where(low, a, pltpu.roll(b, B, 1))
        out_ref[0, B // 2 :, lanes] = jnp.where(low, pltpu.roll(a, B, 1), b)


def params(mib):
    return pltpu.CompilerParams(vmem_limit_bytes=mib * 2**20)


def specs(*spaces):
    return [pl.BlockSpec(memory_space=s) for s in spaces]


def on_device(
    a_blocks, a_cols, p_blocks, contrib_peer, contrib_slot, outbound_term_lists, send_count, keep
):
    rows = lax.axis_size("row")
    columns = lax.axis_size("col")
    own_row = lax.axis_index("row")
    own_col = lax.axis_index("col")
    prolong = p_blocks[0]
    ends = columns - 1
    left = lax.ppermute(prolong[:, -H * B :], "col", [(i, i + 1) for i in range(ends)])
    right = lax.ppermute(prolong[:, : H * B], "col", [(i + 1, i) for i in range(ends)])
    q = pl.pallas_call(
        q_kernel,
        grid=(FB // GROUP,),
        in_specs=[
            pl.BlockSpec((B, GROUP * B), lambda g: (0, g)),
            pl.BlockSpec((GROUP, B, KA * B), lambda g: (g, 0, 0)),
        ],
        out_specs=pl.BlockSpec((GROUP, B, KP * 2 * B), lambda g: (g, 0, 0)),
        out_shape=jax.ShapeDtypeStruct((FB, B, KP * 2 * B), BF16),
        compiler_params=params(24),
        cost_estimate=pl.CostEstimate(flops=10**9, bytes_accessed=15 * 10**6, transcendentals=0),
        name="q_stage",
    )(prolong, a_blocks[0])
    cols = a_cols[0]
    slots = contrib_slot.reshape(FB, KA)
    peers = contrib_peer.reshape(FB, KA)
    outgoing, table, out_slots = pl.pallas_call(
        listed_kernel,
        in_specs=specs(SM, SM, SM, SM, VM, VM, VM, VM),
        out_specs=specs(VM, VM, SM),
        out_shape=[
            jax.ShapeDtypeStruct((N_COL, CAP, B // 2, 2 * B), BF16),
            jax.ShapeDtypeStruct((FB + 2 * H, B, 2 * B), BF16),
            jax.ShapeDtypeStruct((N_COL, CAP), jnp.int32),
        ],
        compiler_params=params(32),
        name="listed_stage",
    )(outbound_term_lists[0], send_count[0], slots, cols, q, prolong, left, right)
    arrived = lax.all_to_all(outgoing, "col", split_axis=0, concat_axis=0, tiled=True)
    arrived_slots = lax.all_to_all(out_slots, "col", split_axis=0, concat_axis=0, tiled=True)
    local_slots = jnp.where(peers == own_col, slots, CS)
    even, odd = pl.pallas_call(
        local_kernel,
        in_specs=specs(SM, SM, VM, VM),
        out_specs=specs(VM, VM),
        out_shape=[jax.ShapeDtypeStruct((CS + 1, B // 2, 2 * B), F32)] * 2,
        compiler_params=params(32),
        cost_estimate=pl.CostEstimate(flops=2 * 10**10, bytes_accessed=15 * 10**6, transcendentals=0),
        name="local_stage",
    )(local_slots, cols, q, table)
    total, sent = pl.pallas_call(
        merge_kernel,
        in_specs=specs(SM, VM, VM, VM),
        out_specs=specs(VM, VM),
        out_shape=[
            jax.ShapeDtypeStruct((CS, B // 2, 2 * B), F32),
            jax.ShapeDtypeStruct((CS, B // 2, 2 * B), BF16),
        ],
        scratch_shapes=[pltpu.VMEM((CS + 1, B // 2, 2 * B), F32)],
        compiler_params=params(32),
        name="merge_stage",
    )(arrived_slots, even, odd, arrived)
    half = rows // 2
    partner = lax.ppermute(sent, "row", [(i, (i + half) % rows) for i in range(rows)])
    return pl.pallas_call(
        final_kernel,
        in_specs=specs(SM, VM, VM),
        out_specs=pl.BlockSpec(memory_space=VM),
        out_shape=jax.ShapeDtypeStruct((1, B, CS * B), F32),
        compiler_params=params(32),
        name="final_stage",
    )(lax.dynamic_slice(keep, (own_row,), (1,)), total, partner)


def solution(mesh):
    placed = (
        P("row", "col", None, None),
        P("row", "col", None),
        P("row", None, "col"),
        P("row", "col"),
        P("row", "col"),
        P("row", "col", None),
        P("row", "col"),
        P(),
    )
    return jax.shard_map(
        on_device, mesh=mesh, in_specs=placed, out_specs=P("row", None, "col"), check_vma=False
    )
```

time: 489 us -> 91.5 us (0.19)
  local copies, waits for them, and re-layouts: 197 us -> 17.4 us
  waiting for transfers between devices: 179 us -> 22.3 us
  matrix products: 71.1 us -> 0 us
  Pallas kernels: 0 us -> 27.2 us
  starting transfers between devices: 35.1 us -> 22.5 us
    ppermute x9 -> x3, waiting for transfers between devices: 136 us -> 6.13 us  [the longest x1 6.12 us: on_device(): lax.ppermute(sent, 'row', [(i, (i + half) % rows) for i in range(rows)])]
    reshape x12 -> x1, local copies, waits for them, and re-layouts: 92.3 us -> 0.09 us  [on_device(): slots = contrib_slot.reshape(FB, KA)]
    dot_general x7 -> x0, matrix products: 71.1 us -> none  [the longest x2 40 us: block_terms(): jnp.einsum('bia,ikbc->ikac', prolong_own, product, preferred_element_type...]
    another operation x8 -> x0, local copies, waits for them, and re-layouts: 47.9 us -> none  [the longest x2 45.5 us: block_terms(): operator_row_blocks.reshape(fine_rows, block_width, depth, block_width)]
    convert_element_type x2 -> x0, local copies, waits for them, and re-layouts: 37.6 us -> none  [block_terms(): galerkin.astype(jnp.bfloat16)]
    all_to_all x1, waiting for transfers between devices: 42.8 us -> 8.62 us  [on_device(): lax.all_to_all(outgoing, 'col', split_axis=0, concat_axis=0, tiled=True)]
    pallas_call x0 -> x5, Pallas kernels: none -> 27.2 us  [the longest x1 10.3 us: on_device(): pl.pallas_call(local_kernel, in_specs=specs(SM, SM, VM, VM), out_specs=sp...]
    ppermute x9 -> x3, starting transfers between devices: 18.7 us -> 9.12 us  [the longest x1 4.55 us: on_device(): lax.ppermute(prolong[:, -H * B:], 'col', [(i, i + 1) for i in range(ends)])]
  transfers between devices with their start and end apart: 11 -> 5, of which waited for: 4 -> 3; matrix products, arithmetic and copies ran while one was open for 53% -> 4% of each run, Pallas kernels for 0% -> 15%
where the time goes in v1:
time: 91.5 us; the launch traced here: 90.9 us
  Pallas kernels  27.2 us (30%)
  starting transfers between devices  22.5 us (25%)
  waiting for transfers between devices  22.3 us (24%)
  local copies, waits for them, and re-layouts  17.4 us (19%)
  other arithmetic  1.41 us (2%)
    unnamed x24, local copies, waits for them, and re-layouts  15.7 us
    pallas_call x1, Pallas kernels, on_device(): pl.pallas_call(local_kernel, in_specs=specs(SM, SM, VM, VM), out_specs=sp...  10.3 us
    all_to_all x1, starting transfers between devices, on_device(): lax.all_to_all(out_slots, 'col', split_axis=0, concat_axis=0, tiled=True)  9.64 us
    all_to_all x1, waiting for transfers between devices, on_device(): lax.all_to_all(outgoing, 'col', split_axis=0, concat_axis=0, tiled=True)  8.62 us
    pallas_call x1, Pallas kernels, on_device(): pl.pallas_call(listed_kernel, in_specs=specs(SM, SM, SM, SM, VM, VM, VM,...  8.27 us
    all_to_all x1, waiting for transfers between devices, on_device(): lax.all_to_all(out_slots, 'col', split_axis=0, concat_axis=0, tiled=True)  7.54 us
    ppermute x1, waiting for transfers between devices, on_device(): lax.ppermute(sent, 'row', [(i, (i + half) % rows) for i in range(rows)])  6.12 us
    ppermute x1, starting transfers between devices, on_device(): lax.ppermute(prolong[:, -H * B:], 'col', [(i, i + 1) for i in range(ends)])  4.55 us
  transfers between devices with their start and end apart: 5, of which 3 were waited for; matrix products, arithmetic and copies ran while one was open for 4% of the time, Pallas kernels for 15%

profile of v1, /device:TPU:0, one launch (start us, length us, event | category | flops | bytes accessed | tf_op | source)
XLA Modules:
  0.0 90.9 jit_solution(5827698132431377370)
XLA Ops:
  0.0 0.9 fusion
  0.9 1.3 %collective-permute-start.1 = (bf16[64,512]{1,0:T(8,128)(2,1)S(1)}, bf16[64,512]{1,0:T(8,128)(2,1)S(1)}, u32[]{:S(2)}, u32[]{:S(2)}) collective-permute-start(bf16[64,512]{1,0:T(8,128)(2,1)S(1)} %get-tuple-element.19), channel_id=1, source_target_pairs={{1,0},{2,1},{3,2},{4,3},{5,4},{6,5},{7,6},{8,7},{9,8},{10,9},{11,1... | collective-permute-start | bytes 196616 | tf_op jit(solution)/shard_map/ppermute | solution.py:144
  2.2 4.5 %collective-permute-start = (bf16[64,512]{1,0:T(8,128)(2,1)S(1)}, bf16[64,512]{1,0:T(8,128)(2,1)S(1)}, u32[]{:S(2)}, u32[]{:S(2)}) collective-permute-start(bf16[64,512]{1,0:T(8,128)(2,1)S(1)} %get-tuple-element.20), channel_id=1, source_target_pairs={{0,1},{1,2},{2,3},{3,4},{4,5},{5,6},{6,7},{7,8},{8,9},{9,10},{10,1... | collective-permute-start | bytes 196616 | tf_op jit(solution)/shard_map/ppermute | solution.py:143
  6.7 0.7 compare_reduce_fusion
  7.5 0.1 eq.11
  7.6 0.8 copy.11
  8.3 0.7 reduce
  9.0 0.1 reshape.8.slots
  9.1 0.8 copy.12
  9.9 0.0 copy-start.2
  9.9 3.1 %copy-done.2 = bf16[1,32,64,1728]{3,2,1,0:T(8,128)(2,1)S(1)} copy-done((bf16[1,32,64,1728]{3,2,1,0:T(8,128)(2,1)S(1)}, bf16[1,32,64,1728]{3,2,1,0:T(8,128)(2,1)}, u32[]{:S(2)}) %copy-start.2) | copy-done | bytes 7077912
  13.0 0.0 copy-start.3
  13.0 0.9 %copy-done.3 = bf16[1,64,2048]{2,1,0:T(8,128)(2,1)S(1)} copy-done((bf16[1,64,2048]{2,1,0:T(8,128)(2,1)S(1)}, bf16[1,64,2048]{2,1,0:T(8,128)(2,1)}, u32[]{:S(2)}) %copy-start.3) | copy-done | bytes 262168
  14.0 0.0 copy-start.4
  14.0 0.0 copy-start.7
  14.0 3.7 %q_stage.1.q_ref = bf16[32,64,1792]{2,1,0:T(8,128)(2,1)S(1)} custom-call(bf16[64,2048]{1,0:T(8,128)(2,1)S(1)} %bitcast.11, bf16[32,64,1728]{2,1,0:T(8,128)(2,1)S(1)} %bitcast.9), custom_call_target="tpu_custom_call" | custom-call | flops 1000000000 | bytes 15000000 | tf_op jit(solution)/shard_map/q_stage/pallas_call | solution.py:145
  17.7 0.0 collective-permute-done.1.right_ref
  17.7 0.0 collective-permute-done.left_ref
  17.7 0.0 copy-done.4
  17.7 0.0 copy-done.7
  17.7 8.3 %listed_stage.1 = (bf16[16,13,32,128]{3,2,1,0:T(8,128)(2,1)}, bf16[48,64,128]{2,1,0:T(8,128)(2,1)S(1)}, s32[16,13]{1,0:T(8,128)}) custom-call(s32[16,13]{1,0:T(8,128)S(1)} %bitcast.16, s32[16]{0:T(128)S(1)} %bitcast.17, s32[32,27]{1,0:T(8,128)S(1)} %reshape.8.slots, s32[32,27]{1,0:T(8,128)S(1)} %bitcast.13, bf16[32,64,1792]{2,1,0:T(8,128)(2,1)S(1)} %q_stage.1.q_ref, ...), custom_call_target="tpu_custom_call" | custom-call | tf_op jit(solution)/shard_map/listed_stage/pallas_call | solution.py:161
  26.0 0.0 copy-start
  26.0 2.9 %copy-done = bf16[32,64,1792]{2,1,0:T(8,128)(2,1)} copy-done((bf16[32,64,1792]{2,1,0:T(8,128)(2,1)}, bf16[32,64,1792]{2,1,0:T(8,128)(2,1)S(1)}, u32[]{:S(2)}) %copy-start) | copy-done | bytes 7340056
  28.9 0.0 copy-start.8
  28.9 0.9 copy-done.8
  29.8 9.6 %all-to-all-start = ((s32[16,1,13]{2,1,0:T(1,128)}), s32[16,1,13]{2,1,0:T(1,128)S(1)}, u32[]{:S(2)}, u32[]{:S(2)}) async-start(s32[16,1,13]{2,1,0:T(1,128)} %bitcast.6), calls=%async_computation | async-start | bytes 16384 | tf_op jit(solution)/shard_map/all_to_all | solution.py:174
  39.5 7.5 %all-to-all-done = s32[16,1,13]{2,1,0:T(1,128)S(1)} async-done(((s32[16,1,13]{2,1,0:T(1,128)}), s32[16,1,13]{2,1,0:T(1,128)S(1)}, u32[]{:S(2)}, u32[]{:S(2)}) %all-to-all-start) | async-done | bytes 864 | tf_op jit(solution)/shard_map/all_to_all | solution.py:174
  47.0 3.7 %all-to-all-start.1 = ((bf16[16,13,32,128]{3,2,1,0:T(8,128)(2,1)}), bf16[16,13,32,128]{3,2,1,0:T(8,128)(2,1)S(1)}, u32[]{:S(2)}, u32[]{:S(2)}) async-start(bf16[16,13,32,128]{3,2,1,0:T(8,128)(2,1)} %get-tuple-element.16), calls=%async_computation.1 | async-start | bytes 3407872 | tf_op jit(solution)/shard_map/all_to_all | solution.py:173
  50.7 0.0 copy-start.1
  50.7 3.1 %copy-done.1 = bf16[32,64,1792]{2,1,0:T(8,128)(2,1)S(1)} copy-done((bf16[32,64,1792]{2,1,0:T(8,128)(2,1)S(1)}, bf16[32,64,1792]{2,1,0:T(8,128)(2,1)}, u32[]{:S(2)}) %copy-start.1) | copy-done | bytes 7340056
  53.8 0.0 copy-start.9
  53.8 1.1 %copy-done.9 = bf16[48,64,128]{2,1,0:T(8,128)(2,1)S(1)} copy-done((bf16[48,64,128]{2,1,0:T(8,128)(2,1)S(1)}, bf16[48,64,128]{2,1,0:T(8,128)(2,1)}, u32[]{:S(2)}) %copy-start.9) | copy-done | bytes 786456
  55.0 0.0 copy-start.10
  55.0 10.3 %local_stage.1 = (f32[55,32,128]{2,1,0:T(8,128)S(1)}, f32[55,32,128]{2,1,0:T(8,128)S(1)}) custom-call(s32[32,27]{1,0:T(8,128)S(1)} %broadcast_select_fusion.slots, s32[32,27]{1,0:T(8,128)S(1)} %bitcast.14, bf16[32,64,1792]{2,1,0:T(8,128)(2,1)S(1)} %copy-done.1, bf16[48,64,128]{2,1,0:T(8,128)(2,1)S(1)} %copy-done.9), custom_call_target="tpu_custom_call" | custom-call | flops 20000000000 | bytes 15000000 | tf_op jit(solution)/shard_map/local_stage/pallas_call | solution.py:176
  65.3 8.6 %all-to-all-done.1.arrived_ref = bf16[16,13,32,128]{3,2,1,0:T(8,128)(2,1)S(1)} async-done(((bf16[16,13,32,128]{3,2,1,0:T(8,128)(2,1)}), bf16[16,13,32,128]{3,2,1,0:T(8,128)(2,1)S(1)}, u32[]{:S(2)}, u32[]{:S(2)}) %all-to-all-start.1) | async-done | bytes 1703968 | tf_op jit(solution)/shard_map/all_to_all | solution.py:173
  73.9 3.1 %merge_stage.1 = (f32[54,32,128]{2,1,0:T(8,128)S(1)}, bf16[54,32,128]{2,1,0:T(8,128)(2,1)}) custom-call(s32[16,13]{1,0:T(8,128)S(1)} %bitcast.15, f32[55,32,128]{2,1,0:T(8,128)S(1)} %get-tuple-element.14.even_ref, f32[55,32,128]{2,1,0:T(8,128)S(1)} %get-tuple-element.15.odd_ref, bf16[16,13,32,128]{3,2,1,0:T(8,128)(2,1)S(1)} %all-to-all-done.1.arrived_ref), custom_call_target="tpu_custom_call" | custom-call | tf_op jit(solution)/shard_map/merge_stage/pallas_call | solution.py:185
  77.0 0.0 copy-start.5
  77.0 0.9 %copy-done.5 = f32[54,32,128]{2,1,0:T(8,128)} copy-done((f32[54,32,128]{2,1,0:T(8,128)}, f32[54,32,128]{2,1,0:T(8,128)S(1)}, u32[]{:S(2)}) %copy-start.5) | copy-done | bytes 884760
  77.9 3.3 %collective-permute-start.2 = (bf16[54,32,128]{2,1,0:T(8,128)(2,1)}, bf16[54,32,128]{2,1,0:T(8,128)(2,1)S(1)}, u32[]{:S(2)}, u32[]{:S(2)}) collective-permute-start(bf16[54,32,128]{2,1,0:T(8,128)(2,1)} %get-tuple-element.18), channel_id=1, source_target_pairs={{0,64},{16,80},{32,96},{48,112},{64,0},{80,16},{96,32},{112,48},{1... | collective-permute-start | bytes 1327112 | tf_op jit(solution)/shard_map/ppermute | solution.py:198
  81.1 0.0 copy-done.10
  81.1 0.6 dynamic_slice.3.keep
  81.8 6.1 %collective-permute-done.2.partner_ref = bf16[54,32,128]{2,1,0:T(8,128)(2,1)S(1)} collective-permute-done((bf16[54,32,128]{2,1,0:T(8,128)(2,1)}, bf16[54,32,128]{2,1,0:T(8,128)(2,1)S(1)}, u32[]{:S(2)}, u32[]{:S(2)}) %collective-permute-start.2) | collective-permute-done | bytes 442400 | tf_op jit(solution)/shard_map/ppermute | solution.py:198
  87.9 0.0 copy-start.6
  87.9 1.2 %copy-done.6 = f32[54,32,128]{2,1,0:T(8,128)S(1)} copy-done((f32[54,32,128]{2,1,0:T(8,128)S(1)}, f32[54,32,128]{2,1,0:T(8,128)}, u32[]{:S(2)}) %copy-start.6) | copy-done | bytes 884760
  89.1 1.8 %final_stage.1 = f32[1,64,3456]{2,1,0:T(8,128)} custom-call(s32[1]{0:T(128)} %dynamic_slice.3.keep, f32[54,32,128]{2,1,0:T(8,128)S(1)} %copy-done.6, bf16[54,32,128]{2,1,0:T(8,128)(2,1)S(1)} %collective-permute-done.2.partner_ref), custom_call_target="tpu_custom_call" | custom-call | tf_op jit(solution)/shard_map/final_stage/pallas_call | solution.py:199
  (1 shorter events, 0.0 us)
Async XLA Ops:
  0.9 16.8 %collective-permute-start.1 = (bf16[64,512]{1,0:T(8,128)(2,1)S(1)}, bf16[64,512]{1,0:T(8,128)(2,1)S(1)}, u32[]{:S(2)}, u32[]{:S(2)}) collective-permute-start(bf16[64,512]{1,0:T(8,128)(2,1)S(1)} %get-tuple-element.19), channel_id=1, source_target_pairs={{1,0},{2,1},{3,2},{4,3},{5,4},{6,5},{7,6},{8,7},{9,8},{10,9},{11,1... | collective-permute-start | bytes 196616 | tf_op jit(solution)/shard_map/ppermute | solution.py:144
  2.2 15.5 %collective-permute-start = (bf16[64,512]{1,0:T(8,128)(2,1)S(1)}, bf16[64,512]{1,0:T(8,128)(2,1)S(1)}, u32[]{:S(2)}, u32[]{:S(2)}) collective-permute-start(bf16[64,512]{1,0:T(8,128)(2,1)S(1)} %get-tuple-element.20), channel_id=1, source_target_pairs={{0,1},{1,2},{2,3},{3,4},{4,5},{5,6},{6,7},{7,8},{8,9},{9,10},{10,1... | collective-permute-start | bytes 196616 | tf_op jit(solution)/shard_map/ppermute | solution.py:143
  9.9 3.1 %copy-start.2 = (bf16[1,32,64,1728]{3,2,1,0:T(8,128)(2,1)S(1)}, bf16[1,32,64,1728]{3,2,1,0:T(8,128)(2,1)}, u32[]{:S(2)}) copy-start(bf16[1,32,64,1728]{3,2,1,0:T(8,128)(2,1)} %param.8) | copy-start | bytes 21233668
  13.0 0.9 %copy-start.3 = (bf16[1,64,2048]{2,1,0:T(8,128)(2,1)S(1)}, bf16[1,64,2048]{2,1,0:T(8,128)(2,1)}, u32[]{:S(2)}) copy-start(bf16[1,64,2048]{2,1,0:T(8,128)(2,1)} %param.10) | copy-start | bytes 786436
  14.0 3.7 %copy-start.4 = (bf16[1,64,2048]{2,1,0:T(8,128)(2,1)S(1)}, bf16[1,64,2048]{2,1,0:T(8,128)(2,1)}, u32[]{:S(2)}) copy-start(bf16[1,64,2048]{2,1,0:T(8,128)(2,1)} %param.10) | copy-start | bytes 786436
  14.0 3.7 %copy-start.7 = (s32[1,16]{1,0:T(1,128)S(1)}, s32[1,16]{1,0:T(1,128)}, u32[]{:S(2)}) copy-start(s32[1,16]{1,0:T(1,128)} %param.14) | copy-start | bytes 196
  26.0 2.9 %copy-start = (bf16[32,64,1792]{2,1,0:T(8,128)(2,1)}, bf16[32,64,1792]{2,1,0:T(8,128)(2,1)S(1)}, u32[]{:S(2)}) copy-start(bf16[32,64,1792]{2,1,0:T(8,128)(2,1)S(1)} %q_stage.1.q_ref) | copy-start | bytes 22020100
  28.9 0.9 copy-start.8
  29.8 17.2 %all-to-all-start = ((s32[16,1,13]{2,1,0:T(1,128)}), s32[16,1,13]{2,1,0:T(1,128)S(1)}, u32[]{:S(2)}, u32[]{:S(2)}) async-start(s32[16,1,13]{2,1,0:T(1,128)} %bitcast.6), calls=%async_computation | async-start | bytes 16384 | tf_op jit(solution)/shard_map/all_to_all | solution.py:174
  47.0 26.9 %all-to-all-start.1 = ((bf16[16,13,32,128]{3,2,1,0:T(8,128)(2,1)}), bf16[16,13,32,128]{3,2,1,0:T(8,128)(2,1)S(1)}, u32[]{:S(2)}, u32[]{:S(2)}) async-start(bf16[16,13,32,128]{3,2,1,0:T(8,128)(2,1)} %get-tuple-element.16), calls=%async_computation.1 | async-start | bytes 3407872 | tf_op jit(solution)/shard_map/all_to_all | solution.py:173
  50.7 3.1 %copy-start.1 = (bf16[32,64,1792]{2,1,0:T(8,128)(2,1)S(1)}, bf16[32,64,1792]{2,1,0:T(8,128)(2,1)}, u32[]{:S(2)}) copy-start(bf16[32,64,1792]{2,1,0:T(8,128)(2,1)} %copy-done) | copy-start | bytes 22020100
  53.8 1.1 %copy-start.9 = (bf16[48,64,128]{2,1,0:T(8,128)(2,1)S(1)}, bf16[48,64,128]{2,1,0:T(8,128)(2,1)}, u32[]{:S(2)}) copy-start(bf16[48,64,128]{2,1,0:T(8,128)(2,1)} %copy-done.8) | copy-start | bytes 2359300
  55.0 26.2 %copy-start.10 = (s32[8]{0:T(128)S(1)}, s32[8]{0:T(128)}, u32[]{:S(2)}) copy-start(s32[8]{0:T(128)} %param.15) | copy-start | bytes 100
  77.0 0.9 %copy-start.5 = (f32[54,32,128]{2,1,0:T(8,128)}, f32[54,32,128]{2,1,0:T(8,128)S(1)}, u32[]{:S(2)}) copy-start(f32[54,32,128]{2,1,0:T(8,128)S(1)} %get-tuple-element.17.acc_ref) | copy-start | bytes 2654212
  77.9 10.0 %collective-permute-start.2 = (bf16[54,32,128]{2,1,0:T(8,128)(2,1)}, bf16[54,32,128]{2,1,0:T(8,128)(2,1)S(1)}, u32[]{:S(2)}, u32[]{:S(2)}) collective-permute-start(bf16[54,32,128]{2,1,0:T(8,128)(2,1)} %get-tuple-element.18), channel_id=1, source_target_pairs={{0,64},{16,80},{32,96},{48,112},{64,0},{80,16},{96,32},{112,48},{1... | collective-permute-start | bytes 1327112 | tf_op jit(solution)/shard_map/ppermute | solution.py:198
  87.9 1.2 %copy-start.6 = (f32[54,32,128]{2,1,0:T(8,128)S(1)}, f32[54,32,128]{2,1,0:T(8,128)}, u32[]{:S(2)}) copy-start(f32[54,32,128]{2,1,0:T(8,128)} %copy-done.5) | copy-start | bytes 2654212

commit v2 on v0

v2 whole, which is shorter than its diff:
```python
import jax
import jax.numpy as jnp
from jax import lax
from jax.experimental import pallas as pl
from jax.experimental.pallas import tpu as pltpu
from jax.sharding import PartitionSpec as P

B = 64
KA = 27
FB = 32
H = 8
ITEMS = 864
CAP = 13
CS = 54
N_ROW = 8
N_COL = 16
SIDE = 4
KP = 14
W = 2 * B
RR = B // 2
SP = 64
NONE = 63
GROUP = 4
CHUNK_TILES = (0, 8, 14, 21, 27)
CHUNKS = 4
SEND_ROWS = 27 * 16
PER = RR // CHUNKS

F32 = jnp.float32
BF16 = jnp.bfloat16
MESH = pl.DeviceIdType.MESH


def iota(shape, dim):
    return lax.broadcasted_iota(jnp.int32, shape, dim)


def packed(pair):
    return jnp.where(iota((RR, W), 1) < B, pair[:RR], pair[RR:])


def fill_table(table_ref, at, tiles, load):
    for m in range(tiles):
        tile = load(m).astype(F32)
        turned = pltpu.roll(tile, B, 1)
        low = iota(tile.shape, 1) < B
        table_ref[at + 2 * m] = jnp.where(low, tile, turned).astype(BF16)
        table_ref[at + 2 * m + 1] = jnp.where(low, turned, tile).astype(BF16)


def kernel(
    cols,
    items,
    counts,
    slot_scalars,
    keep,
    slot_row,
    peer_row,
    p_ref,
    a_ref,
    out_ref,
    a_buf,
    q_buf,
    table,
    halo_left,
    halo_right,
    stage,
    outgoing,
    arrived,
    terms,
    acc,
    own_hot,
    slot_rows,
    y_out,
    y_in,
    a_sems,
    halo_send,
    halo_recv,
    sends,
    recvs,
    y_send,
    y_recv,
):
    row = lax.axis_index("row")
    col = lax.axis_index("col")
    z = col // SIDE
    x = col % SIDE
    partner = ((row + N_ROW // 2) % N_ROW, col)
    before = (row, (col + N_COL - 1) % N_COL)
    after = (row, (col + 1) % N_COL)

    def a_copy(g):
        part = pl.ds(g * GROUP, GROUP)
        return pltpu.make_async_copy(a_ref.at[0, part], a_buf.at[part], a_sems.at[g])

    @pl.loop(0, FB // GROUP)
    def _(g):
        a_copy(g).start()

    barrier = pltpu.get_barrier_semaphore()

    @pl.loop(1, N_COL)
    def _(d):
        pl.semaphore_signal(
            barrier, inc=1, device_id=(row, (col + d) % N_COL), device_id_type=MESH
        )

    pl.semaphore_signal(barrier, inc=1, device_id=partner, device_id_type=MESH)

    fill_table(table, H, FB // 2, lambda m: p_ref[0, :, m * W : (m + 1) * W])
    own_slots = jnp.where(peer_row[...] == col, slot_row[...], NONE)
    own_hot[...] = jnp.where(own_slots == iota((SP, ITEMS), 0), 1.0, 0.0).astype(BF16)
    arrived[col] = jnp.zeros((SEND_ROWS, W), BF16)

    @pl.loop(0, FB // GROUP)
    def _(g):
        a_copy(g).wait()
        for m in range(GROUP // 2):
            pair = p_ref[0, :, pl.ds(pl.multiple_of((g * (GROUP // 2) + m) * W, W), W)]
            for h in range(2):
                i = g * GROUP + 2 * m + h
                q = lax.dot_general(
                    pair[:, h * B : (h + 1) * B],
                    a_buf[i],
                    (((0,), (0,)), ((), ())),
                    preferred_element_type=F32,
                )
                q = q.astype(BF16)
                for kp in range(KP - 1):
                    q_buf[i * KP + kp] = q[:, kp * W : (kp + 1) * W]
                q_buf[i * KP + KP - 1, :, :B] = q[:, (KP - 1) * W :]
                q_buf[i * KP + KP - 1, :, B:] = jnp.zeros((B, B), BF16)

    pl.semaphore_wait(barrier, N_COL)
    to_after = pltpu.make_async_remote_copy(
        src_ref=p_ref.at[0, :, pl.ds((FB - H) * B, H * B)],
        dst_ref=halo_left,
        send_sem=halo_send.at[0],
        recv_sem=halo_recv.at[0],
        device_id=after,
        device_id_type=MESH,
    )
    to_before = pltpu.make_async_remote_copy(
        src_ref=p_ref.at[0, :, pl.ds(0, H * B)],
        dst_ref=halo_right,
        send_sem=halo_send.at[1],
        recv_sem=halo_recv.at[1],
        device_id=before,
        device_id_type=MESH,
    )
    to_after.start()
    to_before.start()
    to_after.wait()
    to_before.wait()
    has_left = jnp.where(col > 0, 1.0, 0.0).astype(F32)
    has_right = jnp.where(col < N_COL - 1, 1.0, 0.0).astype(F32)
    fill_table(
        table, 0, H // 2, lambda m: halo_left[:, m * W : (m + 1) * W].astype(F32) * has_left
    )
    fill_table(
        table, H + FB, H // 2, lambda m: halo_right[:, m * W : (m + 1) * W].astype(F32) * has_right
    )

    zero = jnp.zeros((B, W), BF16)

    def peer_of(n):
        dz = (2 + n // SIDE) % SIDE
        dx = (2 + n % SIDE) % SIDE
        return ((z + dz) % SIDE) * SIDE + (x + dx) % SIDE

    def source_of(n):
        dz = (2 + n // SIDE) % SIDE
        dx = (2 + n % SIDE) % SIDE
        return ((z + SIDE - dz) % SIDE) * SIDE + (x + SIDE - dx) % SIDE

    def send_copy(chunk, n):
        first, last = CHUNK_TILES[chunk], CHUNK_TILES[chunk + 1]
        part = pl.ds(first * 16, (last - first) * 16)
        peer = peer_of(n)
        return pltpu.make_async_remote_copy(
            src_ref=outgoing.at[peer, part],
            dst_ref=arrived.at[col, part],
            send_sem=sends.at[chunk, n],
            recv_sem=recvs.at[chunk, n],
            device_id=(row, peer),
            device_id_type=MESH,
        )

    def recv_copy(chunk, n):
        first, last = CHUNK_TILES[chunk], CHUNK_TILES[chunk + 1]
        part = pl.ds(first * 16, (last - first) * 16)
        peer = source_of(n)
        return pltpu.make_async_remote_copy(
            src_ref=outgoing.at[peer, part],
            dst_ref=arrived.at[peer, part],
            send_sem=sends.at[chunk, n],
            recv_sem=recvs.at[chunk, n],
            device_id=(row, peer),
            device_id_type=MESH,
        )

    place = (iota((16, W), 0) * 16 + iota((16, W), 1) % 16) % CAP

    def list_terms(n):
        p = peer_of(n)
        tags = jnp.full((16, W), NONE, jnp.int32)
        for j in range(CAP):
            e = items[0, p, j]
            i = e // KA
            k = e - i * KA
            kp = k // 2
            odd = (k - 2 * kp) == 1
            tile = q_buf[i * KP + kp]
            t = table[cols[0, i, k]]
            rhs = jnp.concatenate([jnp.where(odd, zero, t), jnp.where(odd, t, zero)], axis=0)
            g = jnp.dot(tile, rhs, preferred_element_type=F32)
            stage[pl.ds(j, RR, stride=CAP), :] = packed(g)
            slot = jnp.where(j < counts[0, p], slot_scalars[0, e], NONE)
            tags = jnp.where(place == j, slot, tags)
        outgoing[p, pl.ds(0, 16)] = tags.astype(F32).astype(BF16)
        outgoing[p, pl.ds(16, RR * CAP)] = stage[...].astype(BF16)
        send_copy(0, n).start()

    pl.loop(0, 10)(list_terms)
    pl.loop(11, N_COL)(list_terms)
    for chunk in range(1, CHUNKS):
        for span in ((0, 10), (11, N_COL)):

            @pl.loop(*span)
            def _(n):
                send_copy(chunk, n).start()

    @pl.loop(0, FB)
    def _(i):
        for kp in range(KP):
            tile = q_buf[i * KP + kp]
            t0 = table[cols[0, i, 2 * kp]]
            if 2 * kp + 1 < KA:
                t1 = table[cols[0, i, 2 * kp + 1]]
                rhs = jnp.concatenate(
                    [jnp.concatenate([t0, zero], axis=1), jnp.concatenate([zero, t1], axis=1)],
                    axis=0,
                )
            else:
                rhs = jnp.concatenate([t0, zero], axis=0)
            g = jnp.dot(tile, rhs, preferred_element_type=F32)
            terms[pl.ds(i * KA + 2 * kp, RR, stride=ITEMS), :] = packed(g[:, :W])
            if 2 * kp + 1 < KA:
                terms[pl.ds(i * KA + 2 * kp + 1, RR, stride=ITEMS), :] = packed(g[:, W:])

    @pl.loop(0, RR)
    def _(r):
        values = terms[pl.ds(pl.multiple_of(r * ITEMS, 8), ITEMS), :].astype(BF16)
        acc[pl.ds(pl.multiple_of(r * SP, SP), SP), :] = jnp.dot(
            own_hot[...], values, preferred_element_type=F32
        )

    lane = iota((1, 2 * W), 1)

    def y_copy(chunk):
        part = pl.ds(chunk * PER * SP, PER * SP)
        return pltpu.make_async_remote_copy(
            src_ref=y_out.at[part],
            dst_ref=y_in.at[part],
            send_sem=y_send.at[chunk],
            recv_sem=y_recv.at[chunk],
            device_id=partner,
            device_id_type=MESH,
        )

    def merge(chunk):
        for span in ((0, 10), (11, N_COL)):

            @pl.loop(*span)
            def _(n):
                recv_copy(chunk, n).wait_recv()

        if chunk == 0:
            group = iota((16, W), 1) // 16
            for half in range(2):
                rows = jnp.full((16, W), float(NONE), F32)
                for s in range(8):
                    src = half * 8 + s
                    tags = arrived[src, 0:16, :].astype(F32)
                    mine = jnp.logical_and(group == s, src != col)
                    rows = jnp.where(mine, tags, rows)
                slot_rows[:, half * W : (half + 1) * W] = rows
        for tile in range(CHUNK_TILES[chunk], CHUNK_TILES[chunk + 1]):
            if tile == 0:
                continue
            tau = tile - 1
            first = tau * 16 // CAP
            last = (tau * 16 + 15) // CAP
            slots = slot_rows[tau % CAP : tau % CAP + 1, :]
            r_of = (tau * 16 + lane % 16) // CAP
            values = arrived[:, tile * 16 : tile * 16 + 16, :].reshape(2 * W, W)
            for r in range(first, last + 1):
                hot = jnp.where(r_of == r, slots, -1.0)
                hot = (hot == iota((SP, 2 * W), 0).astype(F32)).astype(F32).astype(BF16)
                acc[r * SP : (r + 1) * SP, :] += jnp.dot(
                    hot, values, preferred_element_type=F32
                )
        part = slice(chunk * PER * SP, (chunk + 1) * PER * SP)
        y_out[part, :] = acc[part, :].astype(BF16)
        y_copy(chunk).start()

    weight = keep[row].astype(F32)

    def finish(chunk):
        y_copy(chunk).wait_recv()
        part = slice(chunk * PER * SP, (chunk + 1) * PER * SP)
        acc[part, :] = (acc[part, :] + y_in[part, :].astype(F32)) * weight
        low = iota((PER, W), 1) < B
        at = chunk * PER
        for m in range(CS // 2):
            a = acc[pl.ds(at * SP + 2 * m, PER, stride=SP), :]
            b = acc[pl.ds(at * SP + 2 * m + 1, PER, stride=SP), :]
            lanes = slice(m * W, (m + 1) * W)
            out_ref[0, at : at + PER, lanes] = jnp.where(low, a, pltpu.roll(b, B, 1))
            out_ref[0, RR + at : RR + at + PER, lanes] = jnp.where(low, pltpu.roll(a, B, 1), b)

    for chunk in range(CHUNKS):
        merge(chunk)
        if chunk > 0:
            finish(chunk - 1)
    finish(CHUNKS - 1)
    for chunk in range(CHUNKS):
        y_copy(chunk).wait_send()
        for span in ((0, 10), (11, N_COL)):

            @pl.loop(*span)
            def _(n):
                send_copy(chunk, n).wait_send()


def on_device(
    a_blocks, a_cols, p_blocks, contrib_peer, contrib_slot, outbound_term_lists, send_count, keep
):
    smem = pl.BlockSpec(memory_space=pltpu.SMEM)
    vmem = pl.BlockSpec(memory_space=pltpu.VMEM)
    dma = pltpu.SemaphoreType.DMA
    return pl.pallas_call(
        kernel,
        in_specs=[smem] * 5 + [vmem] * 3 + [pl.BlockSpec(memory_space=pl.ANY)],
        out_specs=vmem,
        out_shape=jax.ShapeDtypeStruct((1, B, CS * B), F32),
        scratch_shapes=[
            pltpu.VMEM((FB, B, KA * B), BF16),
            pltpu.VMEM((FB * KP, B, W), BF16),
            pltpu.VMEM((FB + 2 * H, B, W), BF16),
            pltpu.VMEM((B, H * B), BF16),
            pltpu.VMEM((B, H * B), BF16),
            pltpu.VMEM((RR * CAP, W), F32),
            pltpu.VMEM((N_COL, SEND_ROWS, W), BF16),
            pltpu.VMEM((N_COL, SEND_ROWS, W), BF16),
            pltpu.VMEM((RR * ITEMS, W), F32),
            pltpu.VMEM((RR * SP, W), F32),
            pltpu.VMEM((SP, ITEMS), BF16),
            pltpu.VMEM((16, 2 * W), F32),
            pltpu.VMEM((RR * SP, W), BF16),
            pltpu.VMEM((RR * SP, W), BF16),
            dma((FB // GROUP,)),
            dma((2,)),
            dma((2,)),
            dma((CHUNKS, N_COL)),
            dma((CHUNKS, N_COL)),
            dma((CHUNKS,)),
            dma((CHUNKS,)),
        ],
        compiler_params=pltpu.CompilerParams(
            collective_id=0, has_side_effects=True, vmem_limit_bytes=52 * 2**20
        ),
        name="galerkin",
    )(
        a_cols,
        outbound_term_lists,
        send_count,
        contrib_slot,
        keep,
        contrib_slot,
        contrib_peer,
        p_blocks,
        a_blocks,
    )


def solution(mesh):
    placed = (
        P("row", "col", None, None),
        P("row", "col", None),
        P("row", None, "col"),
        P("row", "col"),
        P("row", "col"),
        P("row", "col", None),
        P("row", "col"),
        P(),
    )
    return jax.shard_map(
        on_device, mesh=mesh, in_specs=placed, out_specs=P("row", None, "col"), check_vma=False
    )
```

time: 489 us -> 64.8 us (0.13)
  local copies, waits for them, and re-layouts: 197 us -> 6.1 us
  waiting for transfers between devices: 179 us -> 0 us
  matrix products: 71.1 us -> 0 us
  Pallas kernels: 0 us -> 58.4 us
  starting transfers between devices: 35.1 us -> 0 us
    ppermute x9 -> x0, waiting for transfers between devices: 136 us -> none  [the longest x7 136 us: from_partner(): return lax.ppermute(value, axis, pairs)]
    reshape x12 -> x0, local copies, waits for them, and re-layouts: 92.3 us -> none  [the longest x2 39.9 us: block_terms(): picked = picked.reshape(fine_rows, depth, block_width, block_width)]
    dot_general x7 -> x0, matrix products: 71.1 us -> none  [the longest x2 40 us: block_terms(): jnp.einsum('bia,ikbc->ikac', prolong_own, product, preferred_element_type...]
    pallas_call x0 -> x1, Pallas kernels: none -> 58.4 us  [on_device(): pl.pallas_call(kernel, in_specs=[smem] * 5 + [vmem] * 3 + [pl.BlockSpec(m...]
    another operation x8 -> x0, local copies, waits for them, and re-layouts: 47.9 us -> none  [the longest x2 45.5 us: block_terms(): operator_row_blocks.reshape(fine_rows, block_width, depth, block_width)]
    all_to_all x2 -> x0, waiting for transfers between devices: 42.8 us -> none  [the longest x1 42.8 us: on_device(): lax.all_to_all(outgoing, 'col', split_axis=0, concat_axis=0, tiled=True)]
    convert_element_type x2 -> x0, local copies, waits for them, and re-layouts: 37.6 us -> none  [block_terms(): galerkin.astype(jnp.bfloat16)]
    ppermute x9 -> x0, starting transfers between devices: 18.7 us -> none  [the longest x7 14 us: from_partner(): return lax.ppermute(value, axis, pairs)]
  transfers between devices with their start and end apart: 11 -> 0, of which waited for: 4 -> 0; matrix products, arithmetic and copies ran while one was open for 53% -> 0% of each run, Pallas kernels for 0% -> 0%
where the time goes in v2:
time: 64.8 us; the launch traced here: 64.5 us
  Pallas kernels  58.4 us (90%)
  local copies, waits for them, and re-layouts  6.1 us (9%)
    pallas_call x1, Pallas kernels, on_device(): pl.pallas_call(kernel, in_specs=[smem] * 5 + [vmem] * 3 + [pl.BlockSpec(m...  58.4 us
    unnamed x13, local copies, waits for them, and re-layouts  6.1 us

profile of v2, /device:TPU:0, one launch (start us, length us, event | category | flops | bytes accessed | tf_op | source)
XLA Modules:
  0.0 64.5 jit_solution(2308904603299382035)
XLA Ops:
  0.0 0.8 %copy.10.items = s32[1,16,13]{2,1,0:T(8,128)S(1)} copy(s32[1,16,13]{1,0,2:T(1,128)} %param.13) | data formatting | bytes 1664 | tf_op args[5]
  0.8 0.8 %copy.9.cols = s32[1,32,27]{2,1,0:T(8,128)S(1)} copy(s32[1,32,27]{1,0,2:T(1,128)} %param.9) | data formatting | bytes 6912 | tf_op args[1]
  1.6 0.0 copy-start
  1.6 0.9 %copy-done = bf16[1,64,2048]{2,1,0:T(8,128)(2,1)S(1)} copy-done((bf16[1,64,2048]{2,1,0:T(8,128)(2,1)S(1)}, bf16[1,64,2048]{2,1,0:T(8,128)(2,1)}, u32[]{:S(2)}) %copy-start) | copy-done | bytes 262168
  2.5 0.0 copy-start.1
  2.5 0.7 %copy-done.1 = s32[1,864]{1,0:T(1,128)S(1)} copy-done((s32[1,864]{1,0:T(1,128)S(1)}, s32[1,864]{1,0:T(1,128)}, u32[]{:S(2)}) %copy-start.1) | copy-done | bytes 3480
  3.2 0.0 copy-start.2
  3.2 0.7 %copy-done.2 = s32[1,864]{1,0:T(1,128)S(1)} copy-done((s32[1,864]{1,0:T(1,128)S(1)}, s32[1,864]{1,0:T(1,128)}, u32[]{:S(2)}) %copy-start.2) | copy-done | bytes 3480
  3.9 0.0 copy-start.3
  3.9 0.7 %copy-done.3 = s32[1,16]{1,0:T(1,128)S(1)} copy-done((s32[1,16]{1,0:T(1,128)S(1)}, s32[1,16]{1,0:T(1,128)}, u32[]{:S(2)}) %copy-start.3) | copy-done | bytes 88
  4.5 0.0 copy-start.4
  4.5 0.7 %copy-done.4 = s32[8]{0:T(128)S(1)} copy-done((s32[8]{0:T(128)S(1)}, s32[8]{0:T(128)}, u32[]{:S(2)}) %copy-start.4) | copy-done | bytes 56
  5.2 58.4 %galerkin.1 = f32[1,64,3456]{2,1,0:T(8,128)S(1)} custom-call(s32[1,32,27]{2,1,0:T(8,128)S(1)} %copy.9.cols, s32[1,16,13]{2,1,0:T(8,128)S(1)} %copy.10.items, s32[1,16]{1,0:T(1,128)S(1)} %copy-done.3, s32[1,864]{1,0:T(1,128)S(1)} %copy-done.1, s32[8]{0:T(128)S(1)} %copy-done.4, s32[1,864]{1,0:T(1,128)S(1)} %copy-done.1, s32[1,864]{1,0:T(1,128)S(1)} %copy-done.2, ...), custom_call_target="tpu_custom_call" | custom-call | tf_op jit(solution)/shard_map/galerkin/pallas_call | solution.py:342
  63.6 0.9 %copy.12 = f32[1,64,3456]{2,1,0:T(8,128)} copy(f32[1,64,3456]{2,1,0:T(8,128)S(1)} %galerkin.1) | data formatting | bytes 1769472
Async XLA Ops:
  1.6 1.0 %copy-start = (bf16[1,64,2048]{2,1,0:T(8,128)(2,1)S(1)}, bf16[1,64,2048]{2,1,0:T(8,128)(2,1)}, u32[]{:S(2)}) copy-start(bf16[1,64,2048]{2,1,0:T(8,128)(2,1)} %p_ref.1) | copy-start | bytes 786436
  2.5 0.7 %copy-start.1 = (s32[1,864]{1,0:T(1,128)S(1)}, s32[1,864]{1,0:T(1,128)}, u32[]{:S(2)}) copy-start(s32[1,864]{1,0:T(1,128)} %slot_row.1) | copy-start | bytes 10372
  3.2 0.7 %copy-start.2 = (s32[1,864]{1,0:T(1,128)S(1)}, s32[1,864]{1,0:T(1,128)}, u32[]{:S(2)}) copy-start(s32[1,864]{1,0:T(1,128)} %peer_row.1) | copy-start | bytes 10372
  3.9 0.7 %copy-start.3 = (s32[1,16]{1,0:T(1,128)S(1)}, s32[1,16]{1,0:T(1,128)}, u32[]{:S(2)}) copy-start(s32[1,16]{1,0:T(1,128)} %counts.1) | copy-start | bytes 196
  4.5 0.7 %copy-start.4 = (s32[8]{0:T(128)S(1)}, s32[8]{0:T(128)}, u32[]{:S(2)}) copy-start(s32[8]{0:T(128)} %keep.1) | copy-start | bytes 100

commit v3 on v2

--- a/solution.py
+++ b/solution.py
@@ -17,14 +17,17 @@
 SIDE = 4
 KP = 14
 W = 2 * B
-RR = B // 2
+WW = 4 * B
+RR = B // 4
 SP = 64
 NONE = 63
 GROUP = 4
-CHUNK_TILES = (0, 8, 14, 21, 27)
+Q_BEFORE = 4
+CHUNK_TILES = (0, 5, 8, 11, 14)
 CHUNKS = 4
-SEND_ROWS = 27 * 16
+SEND_ROWS = 14 * 16
 PER = RR // CHUNKS
+Y_ROWS = 2 * PER * CS
 
 F32 = jnp.float32
 BF16 = jnp.bfloat16
@@ -36,7 +39,11 @@
 
 
 def packed(pair):
-    return jnp.where(iota((RR, W), 1) < B, pair[:RR], pair[RR:])
+    return jnp.where(iota((2 * RR, W), 1) < B, pair[: 2 * RR], pair[2 * RR :])
+
+
+def side_by_side(upper, lower):
+    return jnp.concatenate([upper, lower], axis=1)
 
 
 def fill_table(table_ref, at, tiles, load):
@@ -71,6 +78,7 @@
     acc,
     own_hot,
     slot_rows,
+    y_stage,
     y_out,
     y_in,
     a_sems,
@@ -80,6 +88,7 @@
     recvs,
     y_send,
     y_recv,
+    ready,
 ):
     row = lax.axis_index("row")
     col = lax.axis_index("col")
@@ -99,21 +108,31 @@
 
     barrier = pltpu.get_barrier_semaphore()
 
-    @pl.loop(1, N_COL)
-    def _(d):
-        pl.semaphore_signal(
-            barrier, inc=1, device_id=(row, (col + d) % N_COL), device_id_type=MESH
-        )
-
+    def greet(peer):
+        pl.semaphore_signal(barrier, inc=1, device_id=(row, peer), device_id_type=MESH)
+
+    at_edge = jnp.logical_or(x == 0, x == SIDE - 1)
+
+    @pl.when(x == 0)
+    def _():
+        greet((col + N_COL - 1) % N_COL)
+
+    @pl.when(x == SIDE - 1)
+    def _():
+        greet((col + 1) % N_COL)
+
+    for d in range(1, SIDE):
+        greet(z * SIDE + (x + d) % SIDE)
+    for d in range(1, SIDE):
+        greet(((z + d) % SIDE) * SIDE + x)
     pl.semaphore_signal(barrier, inc=1, device_id=partner, device_id_type=MESH)
 
     fill_table(table, H, FB // 2, lambda m: p_ref[0, :, m * W : (m + 1) * W])
     own_slots = jnp.where(peer_row[...] == col, slot_row[...], NONE)
     own_hot[...] = jnp.where(own_slots == iota((SP, ITEMS), 0), 1.0, 0.0).astype(BF16)
-    arrived[col] = jnp.zeros((SEND_ROWS, W), BF16)
-
-    @pl.loop(0, FB // GROUP)
-    def _(g):
+    arrived[col] = jnp.zeros((SEND_ROWS, WW), BF16)
+
+    def form_q(g):
         a_copy(g).wait()
         for m in range(GROUP // 2):
             pair = p_ref[0, :, pl.ds(pl.multiple_of((g * (GROUP // 2) + m) * W, W), W)]
@@ -131,7 +150,15 @@
                 q_buf[i * KP + KP - 1, :, :B] = q[:, (KP - 1) * W :]
                 q_buf[i * KP + KP - 1, :, B:] = jnp.zeros((B, B), BF16)
 
-    pl.semaphore_wait(barrier, N_COL)
+    pl.loop(0, Q_BEFORE)(form_q)
+    pl.semaphore_wait(barrier, 2 * SIDE - 1 + jnp.where(at_edge, 1, 0))
+    for d in range(1, SIDE):
+        pl.semaphore_signal(
+            ready,
+            inc=1,
+            device_id=(row, ((z + d) % SIDE) * SIDE + x),
+            device_id_type=MESH,
+        )
     to_after = pltpu.make_async_remote_copy(
         src_ref=p_ref.at[0, :, pl.ds((FB - H) * B, H * B)],
         dst_ref=halo_left,
@@ -150,8 +177,10 @@
     )
     to_after.start()
     to_before.start()
+    pl.loop(Q_BEFORE, FB // GROUP)(form_q)
     to_after.wait()
     to_before.wait()
+    pl.semaphore_wait(ready, SIDE - 1)
     has_left = jnp.where(col > 0, 1.0, 0.0).astype(F32)
     has_right = jnp.where(col < N_COL - 1, 1.0, 0.0).astype(F32)
     fill_table(
@@ -199,11 +228,11 @@
             device_id_type=MESH,
         )
 
-    place = (iota((16, W), 0) * 16 + iota((16, W), 1) % 16) % CAP
+    place = (iota((16, WW), 0) * 16 + iota((16, WW), 1) % 16) % CAP
 
     def list_terms(n):
         p = peer_of(n)
-        tags = jnp.full((16, W), NONE, jnp.int32)
+        tags = jnp.full((16, WW), NONE, jnp.int32)
         for j in range(CAP):
             e = items[0, p, j]
             i = e // KA
@@ -214,11 +243,13 @@
             t = table[cols[0, i, k]]
             rhs = jnp.concatenate([jnp.where(odd, zero, t), jnp.where(odd, t, zero)], axis=0)
             g = jnp.dot(tile, rhs, preferred_element_type=F32)
-            stage[pl.ds(j, RR, stride=CAP), :] = packed(g)
+            stage[pl.ds(j, 2 * RR, stride=CAP), :] = packed(g)
             slot = jnp.where(j < counts[0, p], slot_scalars[0, e], NONE)
             tags = jnp.where(place == j, slot, tags)
         outgoing[p, pl.ds(0, 16)] = tags.astype(F32).astype(BF16)
-        outgoing[p, pl.ds(16, RR * CAP)] = stage[...].astype(BF16)
+        outgoing[p, pl.ds(16, RR * CAP)] = side_by_side(
+            stage[: RR * CAP, :], stage[RR * CAP :, :]
+        ).astype(BF16)
         send_copy(0, n).start()
 
     pl.loop(0, 10)(list_terms)
@@ -244,21 +275,26 @@
             else:
                 rhs = jnp.concatenate([t0, zero], axis=0)
             g = jnp.dot(tile, rhs, preferred_element_type=F32)
-            terms[pl.ds(i * KA + 2 * kp, RR, stride=ITEMS), :] = packed(g[:, :W])
+            terms[pl.ds(i * KA + 2 * kp, 2 * RR, stride=ITEMS), :] = packed(g[:, :W])
             if 2 * kp + 1 < KA:
-                terms[pl.ds(i * KA + 2 * kp + 1, RR, stride=ITEMS), :] = packed(g[:, W:])
-
-    @pl.loop(0, RR)
-    def _(r):
-        values = terms[pl.ds(pl.multiple_of(r * ITEMS, 8), ITEMS), :].astype(BF16)
-        acc[pl.ds(pl.multiple_of(r * SP, SP), SP), :] = jnp.dot(
-            own_hot[...], values, preferred_element_type=F32
-        )
-
-    lane = iota((1, 2 * W), 1)
+                terms[pl.ds(i * KA + 2 * kp + 1, 2 * RR, stride=ITEMS), :] = packed(g[:, W:])
+
+    def own_sum(chunk):
+        for r in range(chunk * PER, (chunk + 1) * PER):
+            upper = terms[r * ITEMS : (r + 1) * ITEMS, :]
+            lower = terms[(RR + r) * ITEMS : (RR + r + 1) * ITEMS, :]
+            total = jnp.dot(
+                own_hot[...], side_by_side(upper, lower).astype(BF16), preferred_element_type=F32
+            )
+            acc[r * SP : (r + 1) * SP, :] += total[:, :W]
+            acc[(RR + r) * SP : (RR + r + 1) * SP, :] += total[:, W:]
+
+    acc[...] = jnp.zeros_like(acc)
+
+    lane = iota((1, WW), 1)
 
     def y_copy(chunk):
-        part = pl.ds(chunk * PER * SP, PER * SP)
+        part = pl.ds(chunk * Y_ROWS, Y_ROWS)
         return pltpu.make_async_remote_copy(
             src_ref=y_out.at[part],
             dst_ref=y_in.at[part],
@@ -276,15 +312,13 @@
                 recv_copy(chunk, n).wait_recv()
 
         if chunk == 0:
-            group = iota((16, W), 1) // 16
-            for half in range(2):
-                rows = jnp.full((16, W), float(NONE), F32)
-                for s in range(8):
-                    src = half * 8 + s
-                    tags = arrived[src, 0:16, :].astype(F32)
-                    mine = jnp.logical_and(group == s, src != col)
-                    rows = jnp.where(mine, tags, rows)
-                slot_rows[:, half * W : (half + 1) * W] = rows
+            group = iota((16, WW), 1) // 16
+            rows = jnp.full((16, WW), float(NONE), F32)
+            for src in range(N_COL):
+                tags = arrived[src, 0:16, :].astype(F32)
+                mine = jnp.logical_and(group == src, src != col)
+                rows = jnp.where(mine, tags, rows)
+            slot_rows[...] = rows
         for tile in range(CHUNK_TILES[chunk], CHUNK_TILES[chunk + 1]):
             if tile == 0:
                 continue
@@ -293,33 +327,46 @@
             last = (tau * 16 + 15) // CAP
             slots = slot_rows[tau % CAP : tau % CAP + 1, :]
             r_of = (tau * 16 + lane % 16) // CAP
-            values = arrived[:, tile * 16 : tile * 16 + 16, :].reshape(2 * W, W)
-            for r in range(first, last + 1):
-                hot = jnp.where(r_of == r, slots, -1.0)
-                hot = (hot == iota((SP, 2 * W), 0).astype(F32)).astype(F32).astype(BF16)
-                acc[r * SP : (r + 1) * SP, :] += jnp.dot(
-                    hot, values, preferred_element_type=F32
-                )
-        part = slice(chunk * PER * SP, (chunk + 1) * PER * SP)
-        y_out[part, :] = acc[part, :].astype(BF16)
+            values = arrived[:, tile * 16 : tile * 16 + 16, :].reshape(WW, WW)
+            sub = iota((SP, WW), 0).astype(F32)
+            hot = [
+                jnp.where(jnp.where(r_of == r, slots, -1.0) == sub, 1.0, 0.0).astype(BF16)
+                for r in range(first, last + 1)
+            ]
+            more = jnp.dot(jnp.concatenate(hot, axis=0), values, preferred_element_type=F32)
+            acc[first * SP : (last + 1) * SP, :] += more[:, :W]
+            acc[(RR + first) * SP : (RR + last + 1) * SP, :] += more[:, W:]
+        for h in range(2):
+            for n in range(PER):
+                at = (h * RR + chunk * PER + n) * SP
+                y_stage[(h * PER + n) * CS : (h * PER + n + 1) * CS, :] = acc[at : at + CS, :]
+        y_out[chunk * Y_ROWS : (chunk + 1) * Y_ROWS, :] = y_stage[...].astype(BF16)
         y_copy(chunk).start()
 
     weight = keep[row].astype(F32)
 
     def finish(chunk):
         y_copy(chunk).wait_recv()
-        part = slice(chunk * PER * SP, (chunk + 1) * PER * SP)
-        acc[part, :] = (acc[part, :] + y_in[part, :].astype(F32)) * weight
+        y_stage[...] = y_in[chunk * Y_ROWS : (chunk + 1) * Y_ROWS, :].astype(F32)
+        for h in range(2):
+            for n in range(PER):
+                at = (h * RR + chunk * PER + n) * SP
+                more = y_stage[(h * PER + n) * CS : (h * PER + n + 1) * CS, :]
+                acc[at : at + CS, :] = (acc[at : at + CS, :] + more) * weight
         low = iota((PER, W), 1) < B
         at = chunk * PER
         for m in range(CS // 2):
-            a = acc[pl.ds(at * SP + 2 * m, PER, stride=SP), :]
-            b = acc[pl.ds(at * SP + 2 * m + 1, PER, stride=SP), :]
             lanes = slice(m * W, (m + 1) * W)
-            out_ref[0, at : at + PER, lanes] = jnp.where(low, a, pltpu.roll(b, B, 1))
-            out_ref[0, RR + at : RR + at + PER, lanes] = jnp.where(low, pltpu.roll(a, B, 1), b)
+            for half in range(2):
+                up = half * RR + at
+                a = acc[pl.ds(up * SP + 2 * m, PER, stride=SP), :]
+                b = acc[pl.ds(up * SP + 2 * m + 1, PER, stride=SP), :]
+                out_ref[0, up : up + PER, lanes] = jnp.where(low, a, pltpu.roll(b, B, 1))
+                up = 2 * RR + up
+                out_ref[0, up : up + PER, lanes] = jnp.where(low, pltpu.roll(a, B, 1), b)
 
     for chunk in range(CHUNKS):
+        own_sum(chunk)
         merge(chunk)
         if chunk > 0:
             finish(chunk - 1)
@@ -350,15 +397,16 @@
             pltpu.VMEM((FB + 2 * H, B, W), BF16),
             pltpu.VMEM((B, H * B), BF16),
             pltpu.VMEM((B, H * B), BF16),
-            pltpu.VMEM((RR * CAP, W), F32),
-            pltpu.VMEM((N_COL, SEND_ROWS, W), BF16),
-            pltpu.VMEM((N_COL, SEND_ROWS, W), BF16),
-            pltpu.VMEM((RR * ITEMS, W), F32),
-            pltpu.VMEM((RR * SP, W), F32),
+            pltpu.VMEM((2 * RR * CAP, W), F32),
+            pltpu.VMEM((N_COL, SEND_ROWS, WW), BF16),
+            pltpu.VMEM((N_COL, SEND_ROWS, WW), BF16),
+            pltpu.VMEM((2 * RR * ITEMS, W), F32),
+            pltpu.VMEM((2 * RR * SP, W), F32),
             pltpu.VMEM((SP, ITEMS), BF16),
-            pltpu.VMEM((16, 2 * W), F32),
-            pltpu.VMEM((RR * SP, W), BF16),
-            pltpu.VMEM((RR * SP, W), BF16),
+            pltpu.VMEM((16, WW), F32),
+            pltpu.VMEM((2 * PER * CS, W), F32),
+            pltpu.VMEM((CHUNKS * Y_ROWS, W), BF16),
+            pltpu.VMEM((CHUNKS * Y_ROWS, W), BF16),
             dma((FB // GROUP,)),
             dma((2,)),
             dma((2,)),
@@ -366,6 +414,7 @@
             dma((CHUNKS, N_COL)),
             dma((CHUNKS,)),
             dma((CHUNKS,)),
+            pltpu.SemaphoreType.REGULAR,
         ],
         compiler_params=pltpu.CompilerParams(
             collective_id=0, has_side_effects=True, vmem_limit_bytes=52 * 2**20

time: 64.8 us -> 56.5 us (0.87)
  Pallas kernels: 58.4 us -> 49.5 us
    pallas_call x1, Pallas kernels: 58.4 us -> 49.5 us  [on_device(): pl.pallas_call(kernel, in_specs=[smem] * 5 + [vmem] * 3 + [pl.BlockSpec(m...]
where the time goes in v3:
time: 56.5 us; the launch traced here: 55.6 us
  Pallas kernels  49.5 us (88%)
  local copies, waits for them, and re-layouts  6.1 us (11%)
    pallas_call x1, Pallas kernels, on_device(): pl.pallas_call(kernel, in_specs=[smem] * 5 + [vmem] * 3 + [pl.BlockSpec(m...  49.5 us
    unnamed x13, local copies, waits for them, and re-layouts  6.1 us

profile of v3, /device:TPU:0, one launch (start us, length us, event | category | flops | bytes accessed | tf_op | source)
XLA Modules:
  0.0 55.6 jit_solution(1293334680983790226)
XLA Ops:
  0.0 0.8 %copy.10.items = s32[1,16,13]{2,1,0:T(8,128)S(1)} copy(s32[1,16,13]{1,0,2:T(1,128)} %param.13) | data formatting | bytes 1664 | tf_op args[5]
  0.8 0.8 %copy.9.cols = s32[1,32,27]{2,1,0:T(8,128)S(1)} copy(s32[1,32,27]{1,0,2:T(1,128)} %param.9) | data formatting | bytes 6912 | tf_op args[1]
  1.6 0.0 copy-start
  1.6 0.9 %copy-done = bf16[1,64,2048]{2,1,0:T(8,128)(2,1)S(1)} copy-done((bf16[1,64,2048]{2,1,0:T(8,128)(2,1)S(1)}, bf16[1,64,2048]{2,1,0:T(8,128)(2,1)}, u32[]{:S(2)}) %copy-start) | copy-done | bytes 262168
  2.5 0.0 copy-start.1
  2.5 0.7 %copy-done.1 = s32[1,864]{1,0:T(1,128)S(1)} copy-done((s32[1,864]{1,0:T(1,128)S(1)}, s32[1,864]{1,0:T(1,128)}, u32[]{:S(2)}) %copy-start.1) | copy-done | bytes 3480
  3.2 0.0 copy-start.2
  3.2 0.7 %copy-done.2 = s32[1,864]{1,0:T(1,128)S(1)} copy-done((s32[1,864]{1,0:T(1,128)S(1)}, s32[1,864]{1,0:T(1,128)}, u32[]{:S(2)}) %copy-start.2) | copy-done | bytes 3480
  3.9 0.0 copy-start.3
  3.9 0.7 %copy-done.3 = s32[1,16]{1,0:T(1,128)S(1)} copy-done((s32[1,16]{1,0:T(1,128)S(1)}, s32[1,16]{1,0:T(1,128)}, u32[]{:S(2)}) %copy-start.3) | copy-done | bytes 88
  4.5 0.0 copy-start.4
  4.5 0.7 %copy-done.4 = s32[8]{0:T(128)S(1)} copy-done((s32[8]{0:T(128)S(1)}, s32[8]{0:T(128)}, u32[]{:S(2)}) %copy-start.4) | copy-done | bytes 56
  5.2 49.5 %galerkin.1 = f32[1,64,3456]{2,1,0:T(8,128)S(1)} custom-call(s32[1,32,27]{2,1,0:T(8,128)S(1)} %copy.9.cols, s32[1,16,13]{2,1,0:T(8,128)S(1)} %copy.10.items, s32[1,16]{1,0:T(1,128)S(1)} %copy-done.3, s32[1,864]{1,0:T(1,128)S(1)} %copy-done.1, s32[8]{0:T(128)S(1)} %copy-done.4, s32[1,864]{1,0:T(1,128)S(1)} %copy-done.1, s32[1,864]{1,0:T(1,128)S(1)} %copy-done.2, ...), custom_call_target="tpu_custom_call" | custom-call | tf_op jit(solution)/shard_map/galerkin/pallas_call | solution.py:389
  54.7 0.9 %copy.12 = f32[1,64,3456]{2,1,0:T(8,128)} copy(f32[1,64,3456]{2,1,0:T(8,128)S(1)} %galerkin.1) | data formatting | bytes 1769472
Async XLA Ops:
  1.6 1.0 %copy-start = (bf16[1,64,2048]{2,1,0:T(8,128)(2,1)S(1)}, bf16[1,64,2048]{2,1,0:T(8,128)(2,1)}, u32[]{:S(2)}) copy-start(bf16[1,64,2048]{2,1,0:T(8,128)(2,1)} %p_ref.1) | copy-start | bytes 786436
  2.5 0.7 %copy-start.1 = (s32[1,864]{1,0:T(1,128)S(1)}, s32[1,864]{1,0:T(1,128)}, u32[]{:S(2)}) copy-start(s32[1,864]{1,0:T(1,128)} %slot_row.1) | copy-start | bytes 10372
  3.2 0.7 %copy-start.2 = (s32[1,864]{1,0:T(1,128)S(1)}, s32[1,864]{1,0:T(1,128)}, u32[]{:S(2)}) copy-start(s32[1,864]{1,0:T(1,128)} %peer_row.1) | copy-start | bytes 10372
  3.9 0.7 %copy-start.3 = (s32[1,16]{1,0:T(1,128)S(1)}, s32[1,16]{1,0:T(1,128)}, u32[]{:S(2)}) copy-start(s32[1,16]{1,0:T(1,128)} %counts.1) | copy-start | bytes 196
  4.5 0.7 %copy-start.4 = (s32[8]{0:T(128)S(1)}, s32[8]{0:T(128)}, u32[]{:S(2)}) copy-start(s32[8]{0:T(128)} %keep.1) | copy-start | bytes 100

commit v4 on v3

--- a/solution.py
+++ b/solution.py
@@ -22,6 +22,8 @@
 SP = 64
 NONE = 63
 GROUP = 4
+KS = 32
+TERMS = FB * KS
 Q_BEFORE = 4
 CHUNK_TILES = (0, 5, 8, 11, 14)
 CHUNKS = 4
@@ -56,6 +58,16 @@
 
 
 def kernel(
+    cols_ref,
+    items_ref,
+    counts_ref,
+    slot_ref,
+    keep_ref,
+    peer_ref,
+    p_any,
+    a_ref,
+    out_any,
+    out_ref,
     cols,
     items,
     counts,
@@ -64,8 +76,6 @@
     slot_row,
     peer_row,
     p_ref,
-    a_ref,
-    out_ref,
     a_buf,
     q_buf,
     table,
@@ -74,6 +84,7 @@
     stage,
     outgoing,
     arrived,
+    mixed,
     terms,
     acc,
     own_hot,
@@ -89,6 +100,8 @@
     y_send,
     y_recv,
     ready,
+    in_sems,
+    out_sems,
 ):
     row = lax.axis_index("row")
     col = lax.axis_index("col")
@@ -102,10 +115,6 @@
         part = pl.ds(g * GROUP, GROUP)
         return pltpu.make_async_copy(a_ref.at[0, part], a_buf.at[part], a_sems.at[g])
 
-    @pl.loop(0, FB // GROUP)
-    def _(g):
-        a_copy(g).start()
-
     barrier = pltpu.get_barrier_semaphore()
 
     def greet(peer):
@@ -127,9 +136,47 @@
         greet(((z + d) % SIDE) * SIDE + x)
     pl.semaphore_signal(barrier, inc=1, device_id=partner, device_id_type=MESH)
 
+    fetched = [
+        pltpu.make_async_copy(source, here, in_sems.at[n])
+        for n, (source, here) in enumerate(
+            (
+                (p_any, p_ref),
+                (slot_ref, slot_row),
+                (peer_ref, peer_row),
+                (cols_ref, cols),
+                (items_ref, items),
+                (counts_ref, counts),
+                (slot_ref, slot_scalars),
+                (keep_ref, keep),
+            )
+        )
+    ]
+    for copy in fetched:
+        copy.start()
+
+    @pl.loop(0, FB // GROUP)
+    def _(g):
+        a_copy(g).start()
+
+    for copy in fetched:
+        copy.wait()
+
     fill_table(table, H, FB // 2, lambda m: p_ref[0, :, m * W : (m + 1) * W])
-    own_slots = jnp.where(peer_row[...] == col, slot_row[...], NONE)
-    own_hot[...] = jnp.where(own_slots == iota((SP, ITEMS), 0), 1.0, 0.0).astype(BF16)
+    own_slots = jnp.concatenate(
+        [
+            jnp.where(peer_row[...] == col, slot_row[...], NONE),
+            jnp.full((1, TERMS - ITEMS), NONE, jnp.int32),
+        ],
+        axis=1,
+    )
+    place = iota((1, TERMS), 1)
+    spread = jnp.full((1, TERMS), NONE, jnp.int32)
+    for i in range(FB):
+        inside = jnp.logical_and(place >= i * KS, place < i * KS + KA)
+        moved = pltpu.roll(own_slots, i * (KS - KA), 1) if i else own_slots
+        spread = jnp.where(inside, moved, spread)
+    own_hot[...] = jnp.where(spread == iota((SP, TERMS), 0), 1.0, 0.0).astype(BF16)
+    mixed[...] = jnp.zeros_like(mixed)
     arrived[col] = jnp.zeros((SEND_ROWS, WW), BF16)
 
     def form_q(g):
@@ -234,13 +281,13 @@
         p = peer_of(n)
         tags = jnp.full((16, WW), NONE, jnp.int32)
         for j in range(CAP):
-            e = items[0, p, j]
+            e = items[j, 0, p]
             i = e // KA
             k = e - i * KA
             kp = k // 2
             odd = (k - 2 * kp) == 1
             tile = q_buf[i * KP + kp]
-            t = table[cols[0, i, k]]
+            t = table[cols[k, 0, i]]
             rhs = jnp.concatenate([jnp.where(odd, zero, t), jnp.where(odd, t, zero)], axis=0)
             g = jnp.dot(tile, rhs, preferred_element_type=F32)
             stage[pl.ds(j, 2 * RR, stride=CAP), :] = packed(g)
@@ -261,13 +308,12 @@
             def _(n):
                 send_copy(chunk, n).start()
 
-    @pl.loop(0, FB)
-    def _(i):
+    def own_terms(i, buf):
         for kp in range(KP):
             tile = q_buf[i * KP + kp]
-            t0 = table[cols[0, i, 2 * kp]]
+            t0 = table[cols[2 * kp, 0, i]]
             if 2 * kp + 1 < KA:
-                t1 = table[cols[0, i, 2 * kp + 1]]
+                t1 = table[cols[2 * kp + 1, 0, i]]
                 rhs = jnp.concatenate(
                     [jnp.concatenate([t0, zero], axis=1), jnp.concatenate([zero, t1], axis=1)],
                     axis=0,
@@ -275,16 +321,22 @@
             else:
                 rhs = jnp.concatenate([t0, zero], axis=0)
             g = jnp.dot(tile, rhs, preferred_element_type=F32)
-            terms[pl.ds(i * KA + 2 * kp, 2 * RR, stride=ITEMS), :] = packed(g[:, :W])
+            mixed[pl.ds(buf + 2 * kp, 2 * RR, stride=KS), :] = packed(g[:, :W])
             if 2 * kp + 1 < KA:
-                terms[pl.ds(i * KA + 2 * kp + 1, 2 * RR, stride=ITEMS), :] = packed(g[:, W:])
+                mixed[pl.ds(buf + 2 * kp + 1, 2 * RR, stride=KS), :] = packed(g[:, W:])
+        rows = pl.ds(pl.multiple_of(i * KS, KS), KS)
+        for r in range(2 * RR):
+            terms[r, rows, :] = mixed[buf + r * KS : buf + (r + 1) * KS, :].astype(BF16)
+
+    @pl.loop(0, FB // 2)
+    def _(m):
+        own_terms(2 * m, 0)
+        own_terms(2 * m + 1, 2 * RR * KS)
 
     def own_sum(chunk):
         for r in range(chunk * PER, (chunk + 1) * PER):
-            upper = terms[r * ITEMS : (r + 1) * ITEMS, :]
-            lower = terms[(RR + r) * ITEMS : (RR + r + 1) * ITEMS, :]
             total = jnp.dot(
-                own_hot[...], side_by_side(upper, lower).astype(BF16), preferred_element_type=F32
+                own_hot[...], side_by_side(terms[r], terms[RR + r]), preferred_element_type=F32
             )
             acc[r * SP : (r + 1) * SP, :] += total[:, :W]
             acc[(RR + r) * SP : (RR + r + 1) * SP, :] += total[:, W:]
@@ -365,12 +417,24 @@
                 up = 2 * RR + up
                 out_ref[0, up : up + PER, lanes] = jnp.where(low, pltpu.roll(a, B, 1), b)
 
+    def out_copy(n):
+        part = pl.ds(n * 8, 8)
+        return pltpu.make_async_copy(
+            out_ref.at[0, part], out_any.at[0, part], out_sems.at[n]
+        )
+
     for chunk in range(CHUNKS):
         own_sum(chunk)
         merge(chunk)
-        if chunk > 0:
-            finish(chunk - 1)
-    finish(CHUNKS - 1)
+    for chunk in range(CHUNKS):
+        finish(chunk)
+        if chunk == 1:
+            for n in range(0, 8, 2):
+                out_copy(n).start()
+    for n in range(1, 8, 2):
+        out_copy(n).start()
+    for n in range(8):
+        out_copy(n).wait()
     for chunk in range(CHUNKS):
         y_copy(chunk).wait_send()
         for span in ((0, 10), (11, N_COL)):
@@ -383,15 +447,22 @@
 def on_device(
     a_blocks, a_cols, p_blocks, contrib_peer, contrib_slot, outbound_term_lists, send_count, keep
 ):
-    smem = pl.BlockSpec(memory_space=pltpu.SMEM)
-    vmem = pl.BlockSpec(memory_space=pltpu.VMEM)
     dma = pltpu.SemaphoreType.DMA
     return pl.pallas_call(
         kernel,
-        in_specs=[smem] * 5 + [vmem] * 3 + [pl.BlockSpec(memory_space=pl.ANY)],
-        out_specs=vmem,
+        in_specs=[pl.BlockSpec(memory_space=pl.ANY)] * 8,
+        out_specs=pl.BlockSpec(memory_space=pl.ANY),
         out_shape=jax.ShapeDtypeStruct((1, B, CS * B), F32),
         scratch_shapes=[
+            pltpu.VMEM((1, B, CS * B), F32),
+            pltpu.SMEM((KA, 1, FB), jnp.int32),
+            pltpu.SMEM((CAP, 1, N_COL), jnp.int32),
+            pltpu.SMEM(send_count.shape, jnp.int32),
+            pltpu.SMEM(contrib_slot.shape, jnp.int32),
+            pltpu.SMEM(keep.shape, jnp.int32),
+            pltpu.VMEM(contrib_slot.shape, jnp.int32),
+            pltpu.VMEM(contrib_peer.shape, jnp.int32),
+            pltpu.VMEM(p_blocks.shape, BF16),
             pltpu.VMEM((FB, B, KA * B), BF16),
             pltpu.VMEM((FB * KP, B, W), BF16),
             pltpu.VMEM((FB + 2 * H, B, W), BF16),
@@ -400,9 +471,10 @@
             pltpu.VMEM((2 * RR * CAP, W), F32),
             pltpu.VMEM((N_COL, SEND_ROWS, WW), BF16),
             pltpu.VMEM((N_COL, SEND_ROWS, WW), BF16),
-            pltpu.VMEM((2 * RR * ITEMS, W), F32),
+            pltpu.VMEM((4 * RR * KS, W), F32),
+            pltpu.VMEM((2 * RR, TERMS, W), BF16),
             pltpu.VMEM((2 * RR * SP, W), F32),
-            pltpu.VMEM((SP, ITEMS), BF16),
+            pltpu.VMEM((SP, TERMS), BF16),
             pltpu.VMEM((16, WW), F32),
             pltpu.VMEM((2 * PER * CS, W), F32),
             pltpu.VMEM((CHUNKS * Y_ROWS, W), BF16),
@@ -415,18 +487,19 @@
             dma((CHUNKS,)),
             dma((CHUNKS,)),
             pltpu.SemaphoreType.REGULAR,
+            dma((8,)),
+            dma((8,)),
         ],
         compiler_params=pltpu.CompilerParams(
-            collective_id=0, has_side_effects=True, vmem_limit_bytes=52 * 2**20
+            collective_id=0, has_side_effects=True, vmem_limit_bytes=62 * 2**20
         ),
         name="galerkin",
     )(
-        a_cols,
-        outbound_term_lists,
+        jnp.transpose(a_cols, (2, 0, 1)),
+        jnp.transpose(outbound_term_lists, (2, 0, 1)),
         send_count,
         contrib_slot,
         keep,
-        contrib_slot,
         contrib_peer,
         p_blocks,
         a_blocks,

time: 56.5 us -> 51.3 us (0.908); the launches traced: 55.6 us -> 51.2 us
  local copies, waits for them, and re-layouts: 6.1 us -> 2.14 us
    unnamed x13 -> x1, local copies, waits for them, and re-layouts: 6.1 us -> 2.14 us
where the time goes in v4:
time: 51.3 us; the launch traced here: 51.2 us
  Pallas kernels  49 us (96%)
  local copies, waits for them, and re-layouts  2.14 us (4%)
    pallas_call x1, Pallas kernels, on_device(): pl.pallas_call(kernel, in_specs=[pl.BlockSpec(memory_space=pl.ANY)] * 8,...  49 us
    unnamed x1, local copies, waits for them, and re-layouts  2.14 us

profile of v4, /device:TPU:0, one launch (start us, length us, event | category | flops | bytes accessed | tf_op | source)
XLA Modules:
  0.0 51.2 jit_solution(10156245788832738494)
XLA Ops:
  0.0 49.0 %galerkin.1 = f32[1,64,3456]{2,1,0:T(8,128)} custom-call(s32[27,1,32]{2,1,0:T(1,128)} %bitcast.2, s32[13,1,16]{2,1,0:T(1,128)} %bitcast.3, s32[1,16]{1,0:T(1,128)} %counts_ref.1, s32[1,864]{1,0:T(1,128)} %slot_ref.1, s32[8]{0:T(128)} %keep_ref.1, s32[1,864]{1,0:T(1,128)} %peer_ref.1, bf16[1,64,2048]{2,1,0:T(8,128)(2,1)} %p_any.1, bf16[1,32,64,1728]{3,2,1,0:T(8,128)(2,1)} %a_ref.1), custom_call_target="tpu_custom_call" | custom-call | tf_op jit(solution)/shard_map/galerkin/pallas_call | solution.py:451
  49.0 2.1 %copy.10 = f32[1,64,3456]{2,1,0:T(8,128)} copy(f32[1,64,3456]{2,1,0:T(8,128)} %galerkin.1) | data formatting | bytes 1769472

commit v5 on v4

--- a/solution.py
+++ b/solution.py
@@ -23,6 +23,7 @@
 NONE = 63
 GROUP = 4
 KS = 32
+MS = 40
 TERMS = FB * KS
 Q_BEFORE = 4
 CHUNK_TILES = (0, 5, 8, 11, 14)
@@ -85,6 +86,7 @@
     outgoing,
     arrived,
     mixed,
+    mixed_next,
     terms,
     acc,
     own_hot,
@@ -177,6 +179,7 @@
         spread = jnp.where(inside, moved, spread)
     own_hot[...] = jnp.where(spread == iota((SP, TERMS), 0), 1.0, 0.0).astype(BF16)
     mixed[...] = jnp.zeros_like(mixed)
+    mixed_next[...] = jnp.zeros_like(mixed_next)
     arrived[col] = jnp.zeros((SEND_ROWS, WW), BF16)
 
     def form_q(g):
@@ -308,7 +311,8 @@
             def _(n):
                 send_copy(chunk, n).start()
 
-    def own_terms(i, buf):
+    def own_terms(i, here, there):
+        rows = pl.ds(pl.multiple_of(((i + FB - 1) % FB) * KS, KS), KS)
         for kp in range(KP):
             tile = q_buf[i * KP + kp]
             t0 = table[cols[2 * kp, 0, i]]
@@ -321,17 +325,19 @@
             else:
                 rhs = jnp.concatenate([t0, zero], axis=0)
             g = jnp.dot(tile, rhs, preferred_element_type=F32)
-            mixed[pl.ds(buf + 2 * kp, 2 * RR, stride=KS), :] = packed(g[:, :W])
+            here[pl.ds(2 * kp, 2 * RR, stride=MS), :] = packed(g[:, :W])
             if 2 * kp + 1 < KA:
-                mixed[pl.ds(buf + 2 * kp + 1, 2 * RR, stride=KS), :] = packed(g[:, W:])
-        rows = pl.ds(pl.multiple_of(i * KS, KS), KS)
-        for r in range(2 * RR):
-            terms[r, rows, :] = mixed[buf + r * KS : buf + (r + 1) * KS, :].astype(BF16)
+                here[pl.ds(2 * kp + 1, 2 * RR, stride=MS), :] = packed(g[:, W:])
+            for r in range(2 * RR * kp // KP, 2 * RR * (kp + 1) // KP):
+                terms[r, rows, :] = there[r * MS : r * MS + KS, :].astype(BF16)
 
     @pl.loop(0, FB // 2)
     def _(m):
-        own_terms(2 * m, 0)
-        own_terms(2 * m + 1, 2 * RR * KS)
+        own_terms(2 * m, mixed, mixed_next)
+        own_terms(2 * m + 1, mixed_next, mixed)
+
+    for r in range(2 * RR):
+        terms[r, (FB - 1) * KS : FB * KS, :] = mixed_next[r * MS : r * MS + KS, :].astype(BF16)
 
     def own_sum(chunk):
         for r in range(chunk * PER, (chunk + 1) * PER):
@@ -471,7 +477,8 @@
             pltpu.VMEM((2 * RR * CAP, W), F32),
             pltpu.VMEM((N_COL, SEND_ROWS, WW), BF16),
             pltpu.VMEM((N_COL, SEND_ROWS, WW), BF16),
-            pltpu.VMEM((4 * RR * KS, W), F32),
+            pltpu.VMEM((2 * RR * MS, W), F32),
+            pltpu.VMEM((2 * RR * MS, W), F32),
             pltpu.VMEM((2 * RR, TERMS, W), BF16),
             pltpu.VMEM((2 * RR * SP, W), F32),
             pltpu.VMEM((SP, TERMS), BF16),

time: 51.3 us -> 45.9 us (0.89)
  Pallas kernels: 49 us -> 43.7 us
    pallas_call x1, Pallas kernels: 49 us -> 43.7 us  [on_device(): pl.pallas_call(kernel, in_specs=[pl.BlockSpec(memory_space=pl.ANY)] * 8,...]
where the time goes in v5:
time: 45.9 us; the launch traced here: 45.8 us
  Pallas kernels  43.7 us (95%)
  local copies, waits for them, and re-layouts  2.14 us (5%)
    pallas_call x1, Pallas kernels, on_device(): pl.pallas_call(kernel, in_specs=[pl.BlockSpec(memory_space=pl.ANY)] * 8,...  43.7 us
    unnamed x1, local copies, waits for them, and re-layouts  2.14 us

profile of v5, /device:TPU:0, one launch (start us, length us, event | category | flops | bytes accessed | tf_op | source)
XLA Modules:
  0.0 45.8 jit_solution(4354047805973716918)
XLA Ops:
  0.0 43.7 %galerkin.1 = f32[1,64,3456]{2,1,0:T(8,128)} custom-call(s32[27,1,32]{2,1,0:T(1,128)} %bitcast.2, s32[13,1,16]{2,1,0:T(1,128)} %bitcast.3, s32[1,16]{1,0:T(1,128)} %counts_ref.1, s32[1,864]{1,0:T(1,128)} %slot_ref.1, s32[8]{0:T(128)} %keep_ref.1, s32[1,864]{1,0:T(1,128)} %peer_ref.1, bf16[1,64,2048]{2,1,0:T(8,128)(2,1)} %p_any.1, bf16[1,32,64,1728]{3,2,1,0:T(8,128)(2,1)} %a_ref.1), custom_call_target="tpu_custom_call" | custom-call | tf_op jit(solution)/shard_map/galerkin/pallas_call | solution.py:457
  43.7 2.1 %copy.10 = f32[1,64,3456]{2,1,0:T(8,128)} copy(f32[1,64,3456]{2,1,0:T(8,128)} %galerkin.1) | data formatting | bytes 1769472

commit v6 on v5

--- a/solution.py
+++ b/solution.py
@@ -298,7 +298,7 @@
             tags = jnp.where(place == j, slot, tags)
         outgoing[p, pl.ds(0, 16)] = tags.astype(F32).astype(BF16)
         outgoing[p, pl.ds(16, RR * CAP)] = side_by_side(
-            stage[: RR * CAP, :], stage[RR * CAP :, :]
+            stage[: RR * CAP, :], stage[RR * CAP : 2 * RR * CAP, :]
         ).astype(BF16)
         send_copy(0, n).start()
 
@@ -474,13 +474,13 @@
             pltpu.VMEM((FB + 2 * H, B, W), BF16),
             pltpu.VMEM((B, H * B), BF16),
             pltpu.VMEM((B, H * B), BF16),
-            pltpu.VMEM((2 * RR * CAP, W), F32),
+            pltpu.VMEM((2 * RR * CAP + 16, W), F32),
             pltpu.VMEM((N_COL, SEND_ROWS, WW), BF16),
             pltpu.VMEM((N_COL, SEND_ROWS, WW), BF16),
-            pltpu.VMEM((2 * RR * MS, W), F32),
-            pltpu.VMEM((2 * RR * MS, W), F32),
+            pltpu.VMEM((2 * RR * MS + KS, W), F32),
+            pltpu.VMEM((2 * RR * MS + KS, W), F32),
             pltpu.VMEM((2 * RR, TERMS, W), BF16),
-            pltpu.VMEM((2 * RR * SP, W), F32),
+            pltpu.VMEM((2 * RR * SP + SP, W), F32),
             pltpu.VMEM((SP, TERMS), BF16),
             pltpu.VMEM((16, WW), F32),
             pltpu.VMEM((2 * PER * CS, W), F32),

time: 45.9 us -> 45.9 us (level)
  no operation moved by 1% of the time
where the time goes in v6:
time: 45.9 us; the launch traced here: 45.8 us
  Pallas kernels  43.7 us (95%)
  local copies, waits for them, and re-layouts  2.14 us (5%)
    pallas_call x1, Pallas kernels, on_device(): pl.pallas_call(kernel, in_specs=[pl.BlockSpec(memory_space=pl.ANY)] * 8,...  43.7 us
    unnamed x1, local copies, waits for them, and re-layouts  2.14 us

profile of v6, /device:TPU:0, one launch (start us, length us, event | category | flops | bytes accessed | tf_op | source)
XLA Modules:
  0.0 45.8 jit_solution(14047748676779857979)
XLA Ops:
  0.0 43.7 %galerkin.1 = f32[1,64,3456]{2,1,0:T(8,128)} custom-call(s32[27,1,32]{2,1,0:T(1,128)} %bitcast.2, s32[13,1,16]{2,1,0:T(1,128)} %bitcast.3, s32[1,16]{1,0:T(1,128)} %counts_ref.1, s32[1,864]{1,0:T(1,128)} %slot_ref.1, s32[8]{0:T(128)} %keep_ref.1, s32[1,864]{1,0:T(1,128)} %peer_ref.1, bf16[1,64,2048]{2,1,0:T(8,128)(2,1)} %p_any.1, bf16[1,32,64,1728]{3,2,1,0:T(8,128)(2,1)} %a_ref.1), custom_call_target="tpu_custom_call" | custom-call | tf_op jit(solution)/shard_map/galerkin/pallas_call | solution.py:457
  43.7 2.1 %copy.10 = f32[1,64,3456]{2,1,0:T(8,128)} copy(f32[1,64,3456]{2,1,0:T(8,128)} %galerkin.1) | data formatting | bytes 1769472
